TPU v7x, 32 devices: a whole 2x2x4 slice. The times are simulated.
32 devices in a mesh: gx: 2 (over x), gy: 4 (over y, core), gz: 4 (over z).
Axes of the slice: x: 2, y: 2, z: 4, core: 2. Of those that a mesh axis runs over, the one named last changes fastest.
Arguments:
- thermal_state_values: float32 [32, 128, 512], P('gx', 'gy', 'gz'), may hold values from -6 to 6
- flow_speed_components: float32 [3, 32, 128, 512], P(None, 'gx', 'gy', 'gz'), may hold values from -14 to 14
- thermal_diffusivity_coefficient: float32 [32, 128, 512], P('gx', 'gy', 'gz'), may hold values from 0.1 to 3
- specific_volume: float32 [32, 128, 512], P('gx', 'gy', 'gz'), may hold values from 0.5 to 2
- lower_level_helmholtz_offset: float32 [4, 16, 64], P('gx', 'gy', 'gz'), may hold values from 0.5 to 4
Outputs:
- updated_thermal_state: float32 [32, 128, 512], P('gx', 'gy', 'gz')
- pressure_iterate_values: float32 [32, 128, 512], P('gx', 'gy', 'gz')
- pressure_residual: float32 [32, 128, 512], P('gx', 'gy', 'gz')
All inputs are finite; a program needn't handle non-finite values.
Results may differ from a plain program's by a relative error of at most 0.0003.
Values sent between devices are 32-bit elements; how exact they have to be, the bound alone decides.
A program may use at most 128 MiB of HBM per device.

v0:
```python
import jax
import jax.numpy as jnp
from jax import lax
from jax.sharding import PartitionSpec as P

PITERS = 2
SMOOTH = 3
CHEB_C = 8


CLOCK_STEP_SIZE = 0.0002
HELM_SHIFT = 1.0
FINE_LOW = 0.25
FINE_HIGH = 3.0
COARSE_LOW = 0.07
COARSE_HIGH = 2.0
GLL_POINTS = (
    -1.0,
    -0.8717401485096066,
    -0.5917001814331423,
    -0.2092992179024789,
    0.0,
    0.2092992179024789,
    0.5917001814331423,
    0.8717401485096066,
    1.0,
)


def extended(cells, sides, width):
    for axis, dim in sides:
        count = lax.axis_size(axis)
        ends = count - 1
        head = lax.slice_in_dim(cells, 0, width, axis=dim)
        tail = lax.slice_in_dim(cells, cells.shape[dim] - width, cells.shape[dim], axis=dim)
        cells = jnp.concatenate(
            [
                lax.ppermute(tail, axis, [(i, (i + 1) % count) for i in range(ends)]),
                cells,
                lax.ppermute(head, axis, [((i + 1) % count, i) for i in range(ends)]),
            ],
            axis=dim,
        )
    return cells


def legendre_seven(point):
    p_prev = 1.0
    p_cur = point
    for order_k in range(1, 7):
        p_next = ((2.0 * order_k + 1.0) * point * p_cur - order_k * p_prev) / (order_k + 1.0)
        p_prev = p_cur
        p_cur = p_next
    return p_cur


def gll_tables():
    degree_n = 7
    points = list(GLL_POINTS[:4] + GLL_POINTS[5:])
    legend = [legendre_seven(point) for point in points]
    weights = [2.0 / (degree_n * (degree_n + 1) * value * value) for value in legend]
    derivs = []
    for row_no in range(8):
        row_vals = []
        for col_no in range(8):
            if row_no != col_no:
                row_vals.append(
                    legend[row_no] / (legend[col_no] * (points[row_no] - points[col_no]))
                )
            else:
                row_vals.append(0.0)
        derivs.append(row_vals)
    derivs[0][0] = -degree_n * (degree_n + 1) / 4.0
    derivs[7][7] = degree_n * (degree_n + 1) / 4.0
    return (jnp.asarray(derivs, jnp.float32), jnp.asarray(weights, jnp.float32))


def weight_cube(weights):
    return weights[:, None, None] * weights[None, :, None] * weights[None, None, :]


def pair_pass(padded, direction_index):
    extent = padded.shape[direction_index]
    zero_rim = jnp.zeros_like(lax.slice_in_dim(padded, 0, 1, axis=direction_index))
    shifted_up = jnp.concatenate(
        [lax.slice_in_dim(padded, 1, extent, axis=direction_index), zero_rim], axis=direction_index
    )
    shifted_down = jnp.concatenate(
        [zero_rim, lax.slice_in_dim(padded, 0, extent - 1, axis=direction_index)],
        axis=direction_index,
    )
    position = lax.broadcasted_iota(jnp.int32, padded.shape, direction_index) % 8
    return (
        padded
        + jnp.where(position == 0, shifted_up, 0.0)
        + jnp.where(position == 1, shifted_down, 0.0)
    )


def assemble(values):
    padded = extended(values, (("gx", 1), ("gy", 2), ("gz", 3)), 1)
    for direction_index in range(1, 4):
        padded = pair_pass(padded, direction_index)
    return padded[:, 1:-1, 1:-1, 1:-1]


def assemble_one(values):
    return assemble(values[None])[0]


def make_pair(small_t, length_along_z):
    band_t = jnp.kron(jnp.eye(length_along_z // 8, dtype=jnp.float32), small_t).T
    return (small_t, band_t)


def apply_derivative_matrix(values, tables, direction_index):
    small_t, band_t = tables
    length_along_x, length_along_y, length_along_z = values.shape
    if direction_index == 0:
        blocks = values.reshape(length_along_x // 8, 8, length_along_y * length_along_z)
        result = jnp.einsum("ia,xar->xir", small_t, blocks, precision=lax.Precision.HIGHEST)
        return result.reshape(values.shape)
    if direction_index == 1:
        blocks = values.reshape(length_along_x, length_along_y // 8, 8, length_along_z)
        result = jnp.einsum("ia,pyaz->pyiz", small_t, blocks, precision=lax.Precision.HIGHEST)
        return result.reshape(values.shape)
    result = jnp.dot(
        values.reshape(length_along_x * length_along_y, length_along_z),
        band_t,
        precision=lax.Precision.HIGHEST,
    )
    return result.reshape(values.shape)


def stencil(padded, shift_c):
    centre = padded[1:-1, 1:-1, 1:-1]
    beside_all = padded[2:, 1:-1, 1:-1] + padded[:-2, 1:-1, 1:-1]
    beside_all = beside_all + padded[1:-1, 2:, 1:-1] + padded[1:-1, :-2, 1:-1]
    beside_all = beside_all + padded[1:-1, 1:-1, 2:] + padded[1:-1, 1:-1, :-2]
    return (6.0 + shift_c) * centre - beside_all


def chebyshev(equation_misfit, apply_fn, inv_diag, low_end, high_end, sweeps, keep_resid):
    centre = 0.5 * (high_end + low_end)
    half_span = 0.5 * (high_end - low_end)
    span_ratio = centre / half_span
    rho_old = 1.0 / span_ratio
    direction = equation_misfit * inv_diag * (1.0 / centre)
    solution = direction
    for sweep_no in range(1, sweeps):
        equation_misfit = equation_misfit - apply_fn(direction)
        rho_new = 1.0 / (2.0 * span_ratio - rho_old)
        direction = rho_new * rho_old * direction + 2.0 * rho_new / half_span * (
            equation_misfit * inv_diag
        )
        solution = solution + direction
        rho_old = rho_new
    if keep_resid:
        equation_misfit = equation_misfit - apply_fn(direction)
    return (solution, equation_misfit)


def coarse_solve(coarse_r, lower_level_helmholtz_offset):

    def apply_spread(values):
        padded = extended(values, (("gx", 0), ("gy", 1), ("gz", 2)), 1)
        return stencil(padded, lower_level_helmholtz_offset)

    solution, unused = chebyshev(
        coarse_r,
        apply_spread,
        1.0 / (6.0 + lower_level_helmholtz_offset),
        COARSE_LOW,
        COARSE_HIGH,
        CHEB_C,
        False,
    )
    return solution


def shards(
    thermal_state_values,
    flow_speed_components,
    thermal_diffusivity_coefficient,
    specific_volume,
    lower_level_helmholtz_offset,
):
    derivs, weights = gll_tables()
    length_along_x, length_along_y, length_along_z = thermal_state_values.shape
    blocks_x, blocks_y, blocks_z = lower_level_helmholtz_offset.shape
    interpolation_apply = make_pair(derivs, length_along_z)
    adjoint_interpolation = make_pair(derivs.T, length_along_z)
    square_back = make_pair((derivs * derivs).T, length_along_z)
    cube_w = weight_cube(weights)
    quadrature_coefficient = jnp.tile(cube_w, (blocks_x, blocks_y, blocks_z))
    partial_derivative_stack = [
        apply_derivative_matrix(thermal_state_values, interpolation_apply, direction_index)
        for direction_index in range(3)
    ]
    advect = (
        flow_speed_components[0] * partial_derivative_stack[0]
        + flow_speed_components[1] * partial_derivative_stack[1]
        + flow_speed_components[2] * partial_derivative_stack[2]
    )
    diffuse = apply_derivative_matrix(
        quadrature_coefficient * thermal_diffusivity_coefficient * partial_derivative_stack[0],
        adjoint_interpolation,
        0,
    )
    diffuse = diffuse + apply_derivative_matrix(
        quadrature_coefficient * thermal_diffusivity_coefficient * partial_derivative_stack[1],
        adjoint_interpolation,
        1,
    )
    diffuse = diffuse + apply_derivative_matrix(
        quadrature_coefficient * thermal_diffusivity_coefficient * partial_derivative_stack[2],
        adjoint_interpolation,
        2,
    )
    heat_local = -(quadrature_coefficient * advect) - diffuse
    coef_w = quadrature_coefficient * specific_volume
    jacobi_local = (
        apply_derivative_matrix(coef_w, square_back, 0)
        + apply_derivative_matrix(coef_w, square_back, 1)
        + apply_derivative_matrix(coef_w, square_back, 2)
        + HELM_SHIFT * quadrature_coefficient
    )
    quadrature_lumped_matrix = assemble_one(quadrature_coefficient)
    volumetric_source_strength = assemble_one(heat_local)
    jacobi = assemble_one(jacobi_local)
    updated_thermal_state = (
        thermal_state_values
        + CLOCK_STEP_SIZE * volumetric_source_strength / quadrature_lumped_matrix
    )
    boundary_heat_outflow = apply_derivative_matrix(
        quadrature_coefficient * flow_speed_components[0], adjoint_interpolation, 0
    ) + apply_derivative_matrix(
        quadrature_coefficient * flow_speed_components[1], adjoint_interpolation, 1
    )
    boundary_heat_outflow = boundary_heat_outflow + apply_derivative_matrix(
        quadrature_coefficient * (flow_speed_components[2] + updated_thermal_state),
        adjoint_interpolation,
        2,
    )
    right_side = assemble_one(boundary_heat_outflow)
    inv_jac = 1.0 / jacobi

    def apply_fine(values):
        local_k = apply_derivative_matrix(
            coef_w * apply_derivative_matrix(values, interpolation_apply, 0),
            adjoint_interpolation,
            0,
        )
        local_k = local_k + apply_derivative_matrix(
            coef_w * apply_derivative_matrix(values, interpolation_apply, 1),
            adjoint_interpolation,
            1,
        )
        local_k = local_k + apply_derivative_matrix(
            coef_w * apply_derivative_matrix(values, interpolation_apply, 2),
            adjoint_interpolation,
            2,
        )
        return assemble_one(local_k + HELM_SHIFT * quadrature_coefficient * values)

    row_ids = lax.broadcasted_iota(jnp.int32, (length_along_z, blocks_z), 0) // 8
    col_ids = lax.broadcasted_iota(jnp.int32, (length_along_z, blocks_z), 1)
    summer = jnp.where(row_ids == col_ids, 1.0, 0.0).astype(jnp.float32)
    pressure_iterate_values = jnp.zeros_like(thermal_state_values)
    equation_misfit = right_side
    for iter_no in range(PITERS):
        smooth, resid_s = chebyshev(
            equation_misfit, apply_fine, inv_jac, FINE_LOW, FINE_HIGH, SMOOTH, True
        )
        along_z = jnp.dot(
            (quadrature_coefficient * resid_s).reshape(
                length_along_x * length_along_y, length_along_z
            ),
            summer,
            precision=lax.Precision.HIGHEST,
        )
        coarse_r = along_z.reshape(blocks_x, 8, blocks_y, 8, blocks_z).sum(axis=(1, 3)) / 8.0
        correct = coarse_solve(coarse_r, lower_level_helmholtz_offset)
        expanded = jnp.repeat(jnp.repeat(jnp.repeat(correct, 8, 0), 8, 1), 8, 2)
        prolong = assemble_one(quadrature_coefficient * expanded) / quadrature_lumped_matrix
        pressure_iterate_values = pressure_iterate_values + smooth + prolong
        equation_misfit = resid_s - apply_fine(prolong)
    return (updated_thermal_state, pressure_iterate_values, equation_misfit)


def solution(mesh):
    in_specs = (
        P("gx", "gy", "gz"),
        P(None, "gx", "gy", "gz"),
        P("gx", "gy", "gz"),
        P("gx", "gy", "gz"),
        P("gx", "gy", "gz"),
    )
    out_specs = (P("gx", "gy", "gz"), P("gx", "gy", "gz"), P("gx", "gy", "gz"))
    return jax.shard_map(shards, mesh=mesh, in_specs=in_specs, out_specs=out_specs, check_vma=False)
```

profile of v0, /device:TPU:0, one launch (start us, length us, event | category | flops | bytes accessed | tf_op | source)
XLA Modules:
  0.0 823.3 jit_solution(153513364107556021)
XLA Ops:
  10.3 5.4 collective-permute-start.6
  36.0 4.5 collective-permute-start.18
  54.4 5.9 collective-permute-start.2
  61.7 4.3 collective-permute-start.20
  73.0 4.6 collective-permute-start.22
  78.9 4.6 collective-permute-start.4
  85.3 9.2 %collective-permute-done.4 = f32[1,18,34,1]{3,2,1,0:T(8,128)S(1)} collective-permute-done((f32[1,18,34,1]{3,2,1,0:T(8,128)S(1)}, f32[1,18,34,1]{3,2,1,0:T(8,128)S(1)}, u32[]{:S(2)}, u32[]{:S(2)}) %collective-permute-start.4) | collective-permute-done | bytes 2480 | tf_op jit(solution)/shard_map/ppermute | solution.py:38
  94.5 4.6 collective-permute-done.5
  105.8 4.5 collective-permute-start.12
  128.6 5.9 collective-permute-done.16
  134.4 4.7 collective-permute-done.17
  162.2 6.1 collective-permute-done.28
  168.4 4.7 collective-permute-done.29
  195.7 6.1 collective-permute-done.34
  201.9 4.7 collective-permute-done.35
  235.4 5.0 collective-permute-done.40
  240.4 5.4 collective-permute-done.41
  265.3 4.5 collective-permute-start.47
  286.8 4.8 collective-permute-start.53
  308.5 4.8 collective-permute-start.59
  330.2 4.8 collective-permute-start.65
  352.0 4.8 collective-permute-start.71
  373.7 4.8 collective-permute-start.77
  395.5 4.8 collective-permute-start.83
  419.1 4.2 collective-permute-start.88
  424.6 6.1 collective-permute-done.88
  430.8 4.4 collective-permute-done.89
  445.0 4.3 collective-permute-done.91
  462.1 5.5 collective-permute-done.94
  467.6 4.7 collective-permute-done.95
  504.2 6.1 collective-permute-done.100
  510.3 4.7 collective-permute-done.101
  547.2 5.9 collective-permute-done.106
  553.1 4.7 collective-permute-done.107
  585.8 6.1 collective-permute-done.112
  591.9 4.7 collective-permute-done.113
  613.1 4.5 collective-permute-start.119
  634.6 4.8 collective-permute-start.125
  656.3 4.8 collective-permute-start.131
  678.1 4.8 collective-permute-start.137
  699.8 4.8 collective-permute-start.143
  721.5 4.8 collective-permute-start.149
  743.3 4.8 collective-permute-start.155
  774.2 5.9 collective-permute-done.160
  780.1 4.4 collective-permute-done.161
  793.8 4.3 collective-permute-done.163
  809.2 6.1 collective-permute-done.166
  815.3 4.7 collective-permute-done.167
  (773 shorter events, 573.2 us)
Async XLA Ops:
  9.0 42.7 %collective-permute-start.7 = (f32[1,1,32,128]{3,2,1,0:T(8,128)}, f32[1,1,32,128]{3,2,1,0:T(8,128)S(1)}, u32[]{:S(2)}, u32[]{:S(2)}) collective-permute-start(f32[1,1,32,128]{3,2,1,0:T(8,128)} %get-tuple-element.212), channel_id=1, source_target_pairs={{16,0},{17,1},{18,2},{19,3},{20,4},{21,5},{22,6},{23,7},{24,8},{25... | collective-permute-start | bytes 49160 | tf_op jit(solution)/shard_map/ppermute | solution.py:40
  10.3 39.4 %collective-permute-start.6 = (f32[1,1,32,128]{3,2,1,0:T(8,128)}, f32[1,1,32,128]{3,2,1,0:T(8,128)}, u32[]{:S(2)}, u32[]{:S(2)}) collective-permute-start(f32[1,1,32,128]{3,2,1,0:T(8,128)} %get-tuple-element.213), channel_id=1, source_target_pairs={{0,16},{1,17},{2,18},{3,19},{4,20},{5,21},{6,22},{7,23},{8,24},{9,... | collective-permute-start | bytes 49160 | tf_op jit(solution)/shard_map/ppermute | solution.py:38
  30.0 23.1 %collective-permute-start = (f32[1,1,32,128]{3,2,1,0:T(8,128)}, f32[1,1,32,128]{3,2,1,0:T(8,128)S(1)}, u32[]{:S(2)}, u32[]{:S(2)}) collective-permute-start(f32[1,1,32,128]{3,2,1,0:T(8,128)} %get-tuple-element.214), channel_id=1, source_target_pairs={{0,16},{1,17},{2,18},{3,19},{4,20},{5,21},{6,22},{7,23},{8,24},{9,... | collective-permute-start | bytes 49160 | tf_op jit(solution)/shard_map/ppermute | solution.py:38
  31.2 23.2 %collective-permute-start.1 = (f32[1,1,32,128]{3,2,1,0:T(8,128)}, f32[1,1,32,128]{3,2,1,0:T(8,128)S(1)}, u32[]{:S(2)}, u32[]{:S(2)}) collective-permute-start(f32[1,1,32,128]{3,2,1,0:T(8,128)} %get-tuple-element.215), channel_id=1, source_target_pairs={{16,0},{17,1},{18,2},{19,3},{20,4},{21,5},{22,6},{23,7},{24,8},{25... | collective-permute-start | bytes 49160 | tf_op jit(solution)/shard_map/ppermute | solution.py:40
  36.0 24.3 %collective-permute-start.18 = (f32[1,1,32,128]{3,2,1,0:T(8,128)}, f32[1,1,32,128]{3,2,1,0:T(8,128)S(1)}, u32[]{:S(2)}, u32[]{:S(2)}) collective-permute-start(f32[1,1,32,128]{3,2,1,0:T(8,128)} %get-tuple-element.207), channel_id=1, source_target_pairs={{0,16},{1,17},{2,18},{3,19},{4,20},{5,21},{6,22},{7,23},{8,24},{9,... | collective-permute-start | bytes 49160 | tf_op jit(solution)/shard_map/ppermute | solution.py:38
  49.7 12.0 %collective-permute-start.19 = (f32[1,1,32,128]{3,2,1,0:T(8,128)}, f32[1,1,32,128]{3,2,1,0:T(8,128)S(1)}, u32[]{:S(2)}, u32[]{:S(2)}) collective-permute-start(f32[1,1,32,128]{3,2,1,0:T(8,128)} %get-tuple-element.208), channel_id=1, source_target_pairs={{16,0},{17,1},{18,2},{19,3},{20,4},{21,5},{22,6},{23,7},{24,8},{25... | collective-permute-start | bytes 49160 | tf_op jit(solution)/shard_map/ppermute | solution.py:40
  51.8 14.2 %collective-permute-start.8 = (f32[1,18,1,128]{3,2,1,0:T(1,128)S(1)}, f32[1,18,1,128]{3,2,1,0:T(1,128)S(1)}, u32[]{:S(2)}, u32[]{:S(2)}) collective-permute-start(f32[1,18,1,128]{3,2,1,0:T(1,128)S(1)} %get-tuple-element.183), channel_id=1, source_target_pairs={{0,4},{4,8},{8,12},{1,5},{5,9},{9,13},{2,6},{6,10},{10,14},{3,7},{... | collective-permute-start | bytes 27656 | tf_op jit(solution)/shard_map/ppermute | solution.py:38
  53.1 14.2 %collective-permute-start.9 = (f32[1,18,1,128]{3,2,1,0:T(1,128)S(1)}, f32[1,18,1,128]{3,2,1,0:T(1,128)S(1)}, u32[]{:S(2)}, u32[]{:S(2)}) collective-permute-start(f32[1,18,1,128]{3,2,1,0:T(1,128)S(1)} %get-tuple-element.184), channel_id=1, source_target_pairs={{4,0},{8,4},{12,8},{5,1},{9,5},{13,9},{6,2},{10,6},{14,10},{7,3},{... | collective-permute-start | bytes 27656 | tf_op jit(solution)/shard_map/ppermute | solution.py:40
  54.4 16.6 %collective-permute-start.2 = (f32[1,18,1,128]{3,2,1,0:T(1,128)S(1)}, f32[1,18,1,128]{3,2,1,0:T(1,128)S(1)}, u32[]{:S(2)}, u32[]{:S(2)}) collective-permute-start(f32[1,18,1,128]{3,2,1,0:T(1,128)S(1)} %get-tuple-element.185), channel_id=1, source_target_pairs={{0,4},{4,8},{8,12},{1,5},{5,9},{9,13},{2,6},{6,10},{10,14},{3,7},{... | collective-permute-start | bytes 27656 | tf_op jit(solution)/shard_map/ppermute | solution.py:38
  60.4 12.1 %collective-permute-start.3 = (f32[1,18,1,128]{3,2,1,0:T(1,128)S(1)}, f32[1,18,1,128]{3,2,1,0:T(1,128)S(1)}, u32[]{:S(2)}, u32[]{:S(2)}) collective-permute-start(f32[1,18,1,128]{3,2,1,0:T(1,128)S(1)} %get-tuple-element.186), channel_id=1, source_target_pairs={{4,0},{8,4},{12,8},{5,1},{9,5},{13,9},{6,2},{10,6},{14,10},{7,3},{... | collective-permute-start | bytes 27656 | tf_op jit(solution)/shard_map/ppermute | solution.py:40
  61.7 11.1 %collective-permute-start.20 = (f32[1,18,1,128]{3,2,1,0:T(1,128)S(1)}, f32[1,18,1,128]{3,2,1,0:T(1,128)S(1)}, u32[]{:S(2)}, u32[]{:S(2)}) collective-permute-start(f32[1,18,1,128]{3,2,1,0:T(1,128)S(1)} %get-tuple-element.179), channel_id=1, source_target_pairs={{0,4},{4,8},{8,12},{1,5},{5,9},{9,13},{2,6},{6,10},{10,14},{3,7},{... | collective-permute-start | bytes 27656 | tf_op jit(solution)/shard_map/ppermute | solution.py:38
  66.0 6.8 collective-permute-start.21
  67.6 15.9 %collective-permute-start.10 = (f32[1,18,34,1]{3,2,1,0:T(8,128)S(1)}, f32[1,18,34,1]{3,2,1,0:T(8,128)S(1)}, u32[]{:S(2)}, u32[]{:S(2)}) collective-permute-start(f32[1,18,34,1]{3,2,1,0:T(8,128)S(1)} %get-tuple-element.155), channel_id=1, source_target_pairs={{0,1},{1,2},{2,3},{4,5},{5,6},{6,7},{8,9},{9,10},{10,11},{12,13},{... | collective-permute-start | bytes 7352 | tf_op jit(solution)/shard_map/ppermute | solution.py:38
  71.1 13.7 %collective-permute-start.11 = (f32[1,18,34,1]{3,2,1,0:T(8,128)S(1)}, f32[1,18,34,1]{3,2,1,0:T(8,128)S(1)}, u32[]{:S(2)}, u32[]{:S(2)}) collective-permute-start(f32[1,18,34,1]{3,2,1,0:T(8,128)S(1)} %get-tuple-element.156), channel_id=1, source_target_pairs={{1,0},{2,1},{3,2},{5,4},{6,5},{7,6},{9,8},{10,9},{11,10},{13,12},{... | collective-permute-start | bytes 7352 | tf_op jit(solution)/shard_map/ppermute | solution.py:40
  73.0 26.6 %collective-permute-start.22 = (f32[1,18,34,1]{3,2,1,0:T(8,128)S(1)}, f32[1,18,34,1]{3,2,1,0:T(8,128)S(1)}, u32[]{:S(2)}, u32[]{:S(2)}) collective-permute-start(f32[1,18,34,1]{3,2,1,0:T(8,128)S(1)} %get-tuple-element.151), channel_id=1, source_target_pairs={{0,1},{1,2},{2,3},{4,5},{5,6},{6,7},{8,9},{9,10},{10,11},{12,13},{... | collective-permute-start | bytes 7352 | tf_op jit(solution)/shard_map/ppermute | solution.py:38
  77.6 22.0 %collective-permute-start.23 = (f32[1,18,34,1]{3,2,1,0:T(8,128)S(1)}, f32[1,18,34,1]{3,2,1,0:T(8,128)S(1)}, u32[]{:S(2)}, u32[]{:S(2)}) collective-permute-start(f32[1,18,34,1]{3,2,1,0:T(8,128)S(1)} %get-tuple-element.152), channel_id=1, source_target_pairs={{1,0},{2,1},{3,2},{5,4},{6,5},{7,6},{9,8},{10,9},{11,10},{13,12},{... | collective-permute-start | bytes 7352 | tf_op jit(solution)/shard_map/ppermute | solution.py:40
  78.9 15.6 %collective-permute-start.4 = (f32[1,18,34,1]{3,2,1,0:T(8,128)S(1)}, f32[1,18,34,1]{3,2,1,0:T(8,128)S(1)}, u32[]{:S(2)}, u32[]{:S(2)}) collective-permute-start(f32[1,18,34,1]{3,2,1,0:T(8,128)S(1)} %get-tuple-element.157), channel_id=1, source_target_pairs={{0,1},{1,2},{2,3},{4,5},{5,6},{6,7},{8,9},{9,10},{10,11},{12,13},{... | collective-permute-start | bytes 7352 | tf_op jit(solution)/shard_map/ppermute | solution.py:38
  83.5 15.6 %collective-permute-start.5 = (f32[1,18,34,1]{3,2,1,0:T(8,128)S(1)}, f32[1,18,34,1]{3,2,1,0:T(8,128)S(1)}, u32[]{:S(2)}, u32[]{:S(2)}) collective-permute-start(f32[1,18,34,1]{3,2,1,0:T(8,128)S(1)} %get-tuple-element.158), channel_id=1, source_target_pairs={{1,0},{2,1},{3,2},{5,4},{6,5},{7,6},{9,8},{10,9},{11,10},{13,12},{... | collective-permute-start | bytes 7352 | tf_op jit(solution)/shard_map/ppermute | solution.py:40
  123.5 10.9 %collective-permute-start.16 = (f32[1,18,34,1]{3,2,1,0:T(8,128)S(1)}, f32[1,18,34,1]{3,2,1,0:T(8,128)S(1)}, u32[]{:S(2)}, u32[]{:S(2)}) collective-permute-start(f32[1,18,34,1]{3,2,1,0:T(8,128)S(1)} %get-tuple-element.153), channel_id=1, source_target_pairs={{0,1},{1,2},{2,3},{4,5},{5,6},{6,7},{8,9},{9,10},{10,11},{12,13},{... | collective-permute-start | bytes 7352 | tf_op jit(solution)/shard_map/ppermute | solution.py:38
  127.0 12.2 %collective-permute-start.17 = (f32[1,18,34,1]{3,2,1,0:T(8,128)S(1)}, f32[1,18,34,1]{3,2,1,0:T(8,128)S(1)}, u32[]{:S(2)}, u32[]{:S(2)}) collective-permute-start(f32[1,18,34,1]{3,2,1,0:T(8,128)S(1)} %get-tuple-element.154), channel_id=1, source_target_pairs={{1,0},{2,1},{3,2},{5,4},{6,5},{7,6},{9,8},{10,9},{11,10},{13,12},{... | collective-permute-start | bytes 7352 | tf_op jit(solution)/shard_map/ppermute | solution.py:40
  157.4 10.9 %collective-permute-start.28 = (f32[1,18,34,1]{3,2,1,0:T(8,128)S(1)}, f32[1,18,34,1]{3,2,1,0:T(8,128)S(1)}, u32[]{:S(2)}, u32[]{:S(2)}) collective-permute-start(f32[1,18,34,1]{3,2,1,0:T(8,128)S(1)} %get-tuple-element.147), channel_id=1, source_target_pairs={{0,1},{1,2},{2,3},{4,5},{5,6},{6,7},{8,9},{9,10},{10,11},{12,13},{... | collective-permute-start | bytes 7352 | tf_op jit(solution)/shard_map/ppermute | solution.py:38
  160.9 12.2 %collective-permute-start.29 = (f32[1,18,34,1]{3,2,1,0:T(8,128)S(1)}, f32[1,18,34,1]{3,2,1,0:T(8,128)S(1)}, u32[]{:S(2)}, u32[]{:S(2)}) collective-permute-start(f32[1,18,34,1]{3,2,1,0:T(8,128)S(1)} %get-tuple-element.148), channel_id=1, source_target_pairs={{1,0},{2,1},{3,2},{5,4},{6,5},{7,6},{9,8},{10,9},{11,10},{13,12},{... | collective-permute-start | bytes 7352 | tf_op jit(solution)/shard_map/ppermute | solution.py:40
  192.2 9.7 %collective-permute-start.34 = (f32[1,18,34,1]{3,2,1,0:T(8,128)S(1)}, f32[1,18,34,1]{3,2,1,0:T(8,128)S(1)}, u32[]{:S(2)}, u32[]{:S(2)}) collective-permute-start(f32[1,18,34,1]{3,2,1,0:T(8,128)S(1)} %get-tuple-element.145), channel_id=1, source_target_pairs={{0,1},{1,2},{2,3},{4,5},{5,6},{6,7},{8,9},{9,10},{10,11},{12,13},{... | collective-permute-start | bytes 7352 | tf_op jit(solution)/shard_map/ppermute | solution.py:38
  194.4 12.2 %collective-permute-start.35 = (f32[1,18,34,1]{3,2,1,0:T(8,128)S(1)}, f32[1,18,34,1]{3,2,1,0:T(8,128)S(1)}, u32[]{:S(2)}, u32[]{:S(2)}) collective-permute-start(f32[1,18,34,1]{3,2,1,0:T(8,128)S(1)} %get-tuple-element.146), channel_id=1, source_target_pairs={{1,0},{2,1},{3,2},{5,4},{6,5},{7,6},{9,8},{10,9},{11,10},{13,12},{... | collective-permute-start | bytes 7352 | tf_op jit(solution)/shard_map/ppermute | solution.py:40
  230.4 10.0 %collective-permute-start.40 = (f32[1,18,34,1]{3,2,1,0:T(8,128)}, f32[1,18,34,1]{3,2,1,0:T(8,128)}, u32[]{:S(2)}, u32[]{:S(2)}) collective-permute-start(f32[1,18,34,1]{3,2,1,0:T(8,128)} %get-tuple-element.143), channel_id=1, source_target_pairs={{0,1},{1,2},{2,3},{4,5},{5,6},{6,7},{8,9},{9,10},{10,11},{12,13},{... | collective-permute-start | bytes 7352 | tf_op jit(solution)/shard_map/ppermute | solution.py:38
  233.4 12.5 %collective-permute-start.41 = (f32[1,18,34,1]{3,2,1,0:T(8,128)}, f32[1,18,34,1]{3,2,1,0:T(8,128)}, u32[]{:S(2)}, u32[]{:S(2)}) collective-permute-start(f32[1,18,34,1]{3,2,1,0:T(8,128)} %get-tuple-element.144), channel_id=1, source_target_pairs={{1,0},{2,1},{3,2},{5,4},{6,5},{7,6},{9,8},{10,9},{11,10},{13,12},{... | collective-permute-start | bytes 7352 | tf_op jit(solution)/shard_map/ppermute | solution.py:40
  286.8 6.3 collective-permute-start.53
  308.5 6.3 collective-permute-start.59
  330.2 6.3 collective-permute-start.65
  352.0 6.3 collective-permute-start.71
  373.7 6.3 collective-permute-start.77
  395.5 6.3 collective-permute-start.83
  419.1 11.7 %collective-permute-start.88 = (f32[1,18,34,1]{3,2,1,0:T(8,128)S(1)}, f32[1,18,34,1]{3,2,1,0:T(8,128)S(1)}, u32[]{:S(2)}, u32[]{:S(2)}) collective-permute-start(f32[1,18,34,1]{3,2,1,0:T(8,128)S(1)} %get-tuple-element.141), channel_id=1, source_target_pairs={{0,1},{1,2},{2,3},{4,5},{5,6},{6,7},{8,9},{9,10},{10,11},{12,13},{... | collective-permute-start | bytes 7352 | tf_op jit(solution)/shard_map/ppermute | solution.py:38
  423.3 11.9 %collective-permute-start.89 = (f32[1,18,34,1]{3,2,1,0:T(8,128)S(1)}, f32[1,18,34,1]{3,2,1,0:T(8,128)S(1)}, u32[]{:S(2)}, u32[]{:S(2)}) collective-permute-start(f32[1,18,34,1]{3,2,1,0:T(8,128)S(1)} %get-tuple-element.142), channel_id=1, source_target_pairs={{1,0},{2,1},{3,2},{5,4},{6,5},{7,6},{9,8},{10,9},{11,10},{13,12},{... | collective-permute-start | bytes 7352 | tf_op jit(solution)/shard_map/ppermute | solution.py:40
  455.9 11.7 %collective-permute-start.94 = (f32[1,18,34,1]{3,2,1,0:T(8,128)}, f32[1,18,34,1]{3,2,1,0:T(8,128)S(1)}, u32[]{:S(2)}, u32[]{:S(2)}) collective-permute-start(f32[1,18,34,1]{3,2,1,0:T(8,128)} %get-tuple-element.139), channel_id=1, source_target_pairs={{0,1},{1,2},{2,3},{4,5},{5,6},{6,7},{8,9},{9,10},{10,11},{12,13},{... | collective-permute-start | bytes 7352 | tf_op jit(solution)/shard_map/ppermute | solution.py:38
  459.8 12.5 %collective-permute-start.95 = (f32[1,18,34,1]{3,2,1,0:T(8,128)}, f32[1,18,34,1]{3,2,1,0:T(8,128)}, u32[]{:S(2)}, u32[]{:S(2)}) collective-permute-start(f32[1,18,34,1]{3,2,1,0:T(8,128)} %get-tuple-element.140), channel_id=1, source_target_pairs={{1,0},{2,1},{3,2},{5,4},{6,5},{7,6},{9,8},{10,9},{11,10},{13,12},{... | collective-permute-start | bytes 7352 | tf_op jit(solution)/shard_map/ppermute | solution.py:40
  499.2 11.1 %collective-permute-start.100 = (f32[1,18,34,1]{3,2,1,0:T(8,128)S(1)}, f32[1,18,34,1]{3,2,1,0:T(8,128)S(1)}, u32[]{:S(2)}, u32[]{:S(2)}) collective-permute-start(f32[1,18,34,1]{3,2,1,0:T(8,128)S(1)} %get-tuple-element.137), channel_id=1, source_target_pairs={{0,1},{1,2},{2,3},{4,5},{5,6},{6,7},{8,9},{9,10},{10,11},{12,13},{... | collective-permute-start | bytes 7352 | tf_op jit(solution)/shard_map/ppermute | solution.py:38
  502.9 12.2 %collective-permute-start.101 = (f32[1,18,34,1]{3,2,1,0:T(8,128)S(1)}, f32[1,18,34,1]{3,2,1,0:T(8,128)S(1)}, u32[]{:S(2)}, u32[]{:S(2)}) collective-permute-start(f32[1,18,34,1]{3,2,1,0:T(8,128)S(1)} %get-tuple-element.138), channel_id=1, source_target_pairs={{1,0},{2,1},{3,2},{5,4},{6,5},{7,6},{9,8},{10,9},{11,10},{13,12},{... | collective-permute-start | bytes 7352 | tf_op jit(solution)/shard_map/ppermute | solution.py:40
  543.5 9.6 %collective-permute-start.106 = (f32[1,18,34,1]{3,2,1,0:T(8,128)S(1)}, f32[1,18,34,1]{3,2,1,0:T(8,128)S(1)}, u32[]{:S(2)}, u32[]{:S(2)}) collective-permute-start(f32[1,18,34,1]{3,2,1,0:T(8,128)S(1)} %get-tuple-element.135), channel_id=1, source_target_pairs={{0,1},{1,2},{2,3},{4,5},{5,6},{6,7},{8,9},{9,10},{10,11},{12,13},{... | collective-permute-start | bytes 7352 | tf_op jit(solution)/shard_map/ppermute | solution.py:38
  545.7 12.2 %collective-permute-start.107 = (f32[1,18,34,1]{3,2,1,0:T(8,128)S(1)}, f32[1,18,34,1]{3,2,1,0:T(8,128)S(1)}, u32[]{:S(2)}, u32[]{:S(2)}) collective-permute-start(f32[1,18,34,1]{3,2,1,0:T(8,128)S(1)} %get-tuple-element.136), channel_id=1, source_target_pairs={{1,0},{2,1},{3,2},{5,4},{6,5},{7,6},{9,8},{10,9},{11,10},{13,12},{... | collective-permute-start | bytes 7352 | tf_op jit(solution)/shard_map/ppermute | solution.py:40
  582.2 9.7 %collective-permute-start.112 = (f32[1,18,34,1]{3,2,1,0:T(8,128)S(1)}, f32[1,18,34,1]{3,2,1,0:T(8,128)S(1)}, u32[]{:S(2)}, u32[]{:S(2)}) collective-permute-start(f32[1,18,34,1]{3,2,1,0:T(8,128)S(1)} %get-tuple-element.133), channel_id=1, source_target_pairs={{0,1},{1,2},{2,3},{4,5},{5,6},{6,7},{8,9},{9,10},{10,11},{12,13},{... | collective-permute-start | bytes 7352 | tf_op jit(solution)/shard_map/ppermute | solution.py:38
  584.5 12.2 %collective-permute-start.113 = (f32[1,18,34,1]{3,2,1,0:T(8,128)S(1)}, f32[1,18,34,1]{3,2,1,0:T(8,128)S(1)}, u32[]{:S(2)}, u32[]{:S(2)}) collective-permute-start(f32[1,18,34,1]{3,2,1,0:T(8,128)S(1)} %get-tuple-element.134), channel_id=1, source_target_pairs={{1,0},{2,1},{3,2},{5,4},{6,5},{7,6},{9,8},{10,9},{11,10},{13,12},{... | collective-permute-start | bytes 7352 | tf_op jit(solution)/shard_map/ppermute | solution.py:40
  634.6 6.3 collective-permute-start.125
  656.3 6.3 collective-permute-start.131
  768.5 11.7 %collective-permute-start.160 = (f32[1,18,34,1]{3,2,1,0:T(8,128)S(1)}, f32[1,18,34,1]{3,2,1,0:T(8,128)S(1)}, u32[]{:S(2)}, u32[]{:S(2)}) collective-permute-start(f32[1,18,34,1]{3,2,1,0:T(8,128)S(1)} %get-tuple-element.131), channel_id=1, source_target_pairs={{0,1},{1,2},{2,3},{4,5},{5,6},{6,7},{8,9},{9,10},{10,11},{12,13},{... | collective-permute-start | bytes 7352 | tf_op jit(solution)/shard_map/ppermute | solution.py:38
  772.7 11.9 %collective-permute-start.161 = (f32[1,18,34,1]{3,2,1,0:T(8,128)S(1)}, f32[1,18,34,1]{3,2,1,0:T(8,128)S(1)}, u32[]{:S(2)}, u32[]{:S(2)}) collective-permute-start(f32[1,18,34,1]{3,2,1,0:T(8,128)S(1)} %get-tuple-element.132), channel_id=1, source_target_pairs={{1,0},{2,1},{3,2},{5,4},{6,5},{7,6},{9,8},{10,9},{11,10},{13,12},{... | collective-permute-start | bytes 7352 | tf_op jit(solution)/shard_map/ppermute | solution.py:40
  803.9 11.4 %collective-permute-start.166 = (f32[1,18,34,1]{3,2,1,0:T(8,128)S(1)}, f32[1,18,34,1]{3,2,1,0:T(8,128)S(1)}, u32[]{:S(2)}, u32[]{:S(2)}) collective-permute-start(f32[1,18,34,1]{3,2,1,0:T(8,128)S(1)} %get-tuple-element.129), channel_id=1, source_target_pairs={{0,1},{1,2},{2,3},{4,5},{5,6},{6,7},{8,9},{9,10},{10,11},{12,13},{... | collective-permute-start | bytes 7352 | tf_op jit(solution)/shard_map/ppermute | solution.py:38
  807.9 12.2 %collective-permute-start.167 = (f32[1,18,34,1]{3,2,1,0:T(8,128)S(1)}, f32[1,18,34,1]{3,2,1,0:T(8,128)S(1)}, u32[]{:S(2)}, u32[]{:S(2)}) collective-permute-start(f32[1,18,34,1]{3,2,1,0:T(8,128)S(1)} %get-tuple-element.130), channel_id=1, source_target_pairs={{1,0},{2,1},{3,2},{5,4},{6,5},{7,6},{9,8},{10,9},{11,10},{13,12},{... | collective-permute-start | bytes 7352 | tf_op jit(solution)/shard_map/ppermute | solution.py:40
  (172 other events, 1293.7 us)
where the time goes:
time: 837 us; the launch traced here: 823 us
  starting transfers between devices  337 us (40%)
  waiting for transfers between devices  334 us (40%)
  local copies, waits for them, and re-layouts  54.2 us (6%)
  matrix products  47.1 us (6%)
  other arithmetic  45.3 us (5%)
    ppermute x84, waiting for transfers between devices, extended(): lax.ppermute(head, axis, [((i + 1) % count, i) for i in range(ends)])  238 us
    ppermute x84, starting transfers between devices, extended(): lax.ppermute(tail, axis, [(i, (i + 1) % count) for i in range(ends)])  228 us
    ppermute x84, starting transfers between devices, extended(): lax.ppermute(head, axis, [((i + 1) % count, i) for i in range(ends)])  110 us
    ppermute x84, waiting for transfers between devices, extended(): lax.ppermute(tail, axis, [(i, (i + 1) % count) for i in range(ends)])  95.6 us
    dot_general x20, matrix products, apply_derivative_matrix(): jnp.dot(values.reshape(length_along_x * length_along_y, length_along_z),...  18.8 us
    dot_general x20, matrix products, apply_derivative_matrix(): jnp.einsum('ia,pyaz->pyiz', small_t, blocks, precision=lax.Precision.HIGH...  17.7 us
  transfers between devices with their start and end apart: 168, of which 99 were waited for; matrix products, arithmetic and copies ran while one was open for 4% of the time, Pallas kernels for 0%

commit v1 on v0

v1 whole, which is shorter than its diff:
```python
import functools
import itertools

import jax
import jax.numpy as jnp
import numpy as np
from jax import lax
from jax.experimental import pallas as pl
from jax.experimental.pallas import tpu as pltpu
from jax.sharding import PartitionSpec as P

PITERS = 2
SMOOTH = 3
CHEB_C = 8
CLOCK_STEP_SIZE = 0.0002
HELM_SHIFT = 1.0
FINE_LOW = 0.25
FINE_HIGH = 3.0
COARSE_LOW = 0.07
COARSE_HIGH = 2.0
GLL_POINTS = (
    -1.0,
    -0.8717401485096066,
    -0.5917001814331423,
    -0.2092992179024789,
    0.2092992179024789,
    0.5917001814331423,
    0.8717401485096066,
    1.0,
)
MESH = pl.DeviceIdType.MESH
HIGHEST = lax.Precision.HIGHEST
F32 = jnp.float32
OFFSETS = [o for o in itertools.product((-1, 0, 1), repeat=3) if o != (0, 0, 0)]
SLOT_OF = {o: n for n, o in enumerate(OFFSETS)}


def legendre_seven(point):
    p_prev = 1.0
    p_cur = point
    for order_k in range(1, 7):
        p_next = ((2.0 * order_k + 1.0) * point * p_cur - order_k * p_prev) / (order_k + 1.0)
        p_prev = p_cur
        p_cur = p_next
    return p_cur


def gll_tables():
    points = GLL_POINTS
    legend = [legendre_seven(point) for point in points]
    weights = [2.0 / (56.0 * value * value) for value in legend]
    derivs = np.zeros((8, 8))
    for i in range(8):
        for a in range(8):
            if i != a:
                derivs[i, a] = legend[i] / (legend[a] * (points[i] - points[a]))
    derivs[0, 0] = -14.0
    derivs[7, 7] = 14.0
    return derivs.astype(np.float32), np.asarray(weights, np.float32)


def dot(a, b, dims=((1,), (0,))):
    return lax.dot_general(a, b, (dims, ((), ())), precision=HIGHEST, preferred_element_type=F32)


def fine_coefficients():
    centre = 0.5 * (FINE_HIGH + FINE_LOW)
    half = 0.5 * (FINE_HIGH - FINE_LOW)
    ratio = centre / half
    rho = 1.0 / ratio
    steps = []
    for _ in range(1, SMOOTH):
        new = 1.0 / (2.0 * ratio - rho)
        steps.append((new * rho, 2.0 * new / half))
        rho = new
    return 1.0 / centre, steps


def kernel(
    sizes,
    blocks,
    temp_ref,
    flow_ref,
    cond_ref,
    vol_ref,
    off_ref,
    gz_ref,
    ky_ref,
    wyz_ref,
    wcol_ref,
    wrow_ref,
    newt_ref,
    press_ref,
    resid_ref,
    weight,
    coef,
    q,
    direc,
    part,
    ysend,
    zsend,
    xrecv,
    yrecv,
    zrecv,
    place,
    csend,
    cgrid,
    padded,
    pz,
    pxy,
    restr,
    send_sem,
    recv_sem,
    gsend_sem,
    grecv_sem,
):
    derivs, weights = gll_tables()
    nx, ny, nz = sizes
    bx, by, bz = blocks
    lx, ly, lz = 8 * bx, 8 * by, 8 * bz
    rows = 8 * ly
    devices = nx * ny * nz
    grid_x, grid_y, grid_z = nx * bx, ny * by, nz * bz
    ix, iy, iz = lax.axis_index("gx"), lax.axis_index("gy"), lax.axis_index("gz")
    me = (ix * ny + iy) * nz + iz

    def coords(linear):
        return (linear // (ny * nz), (linear // nz) % ny, linear % nz)

    xrecv[...] = jnp.zeros(xrecv.shape, F32)
    yrecv[...] = jnp.zeros(yrecv.shape, F32)
    zrecv[...] = jnp.zeros(zrecv.shape, F32)

    barrier = pltpu.get_barrier_semaphore()

    def greet(n, carry):
        pl.semaphore_signal(
            barrier, inc=1, device_id=coords(lax.rem(me + n, devices)), device_id_type=MESH
        )
        return carry

    lax.fori_loop(1, devices, greet, 0)

    lane = lax.broadcasted_iota(jnp.int32, (rows, lz), 1)
    row_y = lax.broadcasted_iota(jnp.int32, (rows, lz), 0) % ly
    z_up = (lane % 8 == 7) & (lane < lz - 1)
    z_down = (lane % 8 == 0) & (lane > 0)
    y_up = (row_y % 8 == 7) & (row_y < ly - 1)
    y_down = (row_y % 8 == 0) & (row_y > 0)

    for x in range(lx):
        weight[x] = wyz_ref[...] * float(weights[x % 8])
    coef[...] = weight[...] * vol_ref[...]

    def share(node, elements, element):
        owner = node // 8
        local = node % 8
        low = (local == 0) & (owner > 0)
        high = (local == 7) & (owner < elements - 1)
        here = jnp.where(low | high, 0.5, 1.0)
        there = (low & (element == owner - 1)) | (high & (element == owner + 1))
        return jnp.where(element == owner, here, jnp.where(there, 0.5, 0.0))

    pz[...] = share(
        lax.broadcasted_iota(jnp.int32, (128, lz), 1) + iz * lz,
        grid_z,
        lax.broadcasted_iota(jnp.int32, (128, lz), 0),
    )
    node = lax.broadcasted_iota(jnp.int32, (lx * ly, grid_x * grid_y), 0)
    elem = lax.broadcasted_iota(jnp.int32, (lx * ly, grid_x * grid_y), 1)
    pxy[...] = share(node // ly + ix * lx, grid_x, elem // grid_y) * share(
        node % ly + iy * ly, grid_y, elem % grid_y
    )
    here = lax.broadcasted_iota(jnp.int32, (lz, 128), 0) // 8 + iz * bz
    restr[...] = jnp.where(
        here == lax.broadcasted_iota(jnp.int32, (lz, 128), 1), wcol_ref[...] * 0.125, 0.0
    )

    gz_t, gz, gz_sq = gz_ref[0], gz_ref[1], gz_ref[2]

    def along_x(v, matrix):
        layers = [v[a * ly : (a + 1) * ly] for a in range(8)]
        out = []
        for i in range(8):
            acc = layers[0] * float(matrix[i, 0])
            for a in range(1, 8):
                acc = acc + layers[a] * float(matrix[i, a])
            out.append(acc)
        return jnp.concatenate(out, axis=0)

    def block(ref, b, lead=None):
        if lead is None:
            return ref[8 * b : 8 * b + 8].reshape(rows, lz)
        return ref[lead, 8 * b : 8 * b + 8].reshape(rows, lz)

    def assemble_block(v):
        v = (
            v
            + jnp.where(z_up, pltpu.roll(v, lz - 1, 1), 0.0)
            + jnp.where(z_down, pltpu.roll(v, 1, 1), 0.0)
        )
        return (
            v
            + jnp.where(y_up, pltpu.roll(v, rows - 1, 0), 0.0)
            + jnp.where(y_down, pltpu.roll(v, 1, 0), 0.0)
        )

    ends = (lax.broadcasted_iota(jnp.int32, (8, lz), 0) == 0) & (
        lax.broadcasted_iota(jnp.int32, (8, lz), 1) == 0
    )
    ends = ends | (
        (lax.broadcasted_iota(jnp.int32, (8, lz), 0) == 1)
        & (lax.broadcasted_iota(jnp.int32, (8, lz), 1) == lz - 1)
    )
    ends = jnp.where(ends, 1.0, 0.0).astype(F32)

    def neighbour(o):
        to = (ix + o[0], iy + o[1], iz + o[2])
        there = None
        for value, size, step in zip(to, sizes, o):
            if step:
                ok = (value >= 0) if step < 0 else (value < size)
                there = ok if there is None else (there & ok)
        return to, there

    def buffers(o, slot):
        ox, oy, oz = o
        if oz:
            out = zsend.at[slot, (oz + 1) // 2]
        elif oy:
            out = ysend.at[slot, (oy + 1) // 2]
        else:
            out = part.at[slot, 0 if ox < 0 else lx - 1]

        def land(p):
            px, py, pz_ = p
            if pz_:
                return zrecv.at[slot, (pz_ + 1) // 2, py + 1, px + 1]
            if py:
                return yrecv.at[slot, (py + 1) // 2, px + 1]
            return xrecv.at[slot, (px + 1) // 2]

        return out, land

    def exists(o):
        return all(s > 1 or not d for s, d in zip(sizes, o))

    def sending(o, slot):
        back = tuple(-d for d in o)
        out, land = buffers(o, slot)
        return pltpu.make_async_remote_copy(
            src_ref=out,
            dst_ref=land(back),
            send_sem=send_sem.at[slot, SLOT_OF[o]],
            recv_sem=recv_sem.at[slot, SLOT_OF[back]],
            device_id=neighbour(o)[0],
            device_id_type=MESH,
        )

    def receiving(o, slot):
        out, land = buffers(o, slot)
        return pltpu.make_async_remote_copy(
            src_ref=out,
            dst_ref=land(o),
            send_sem=send_sem.at[slot, SLOT_OF[o]],
            recv_sem=recv_sem.at[slot, SLOT_OF[o]],
            device_id=neighbour(o)[0],
            device_id_type=MESH,
        )

    def begin(slot, fields):
        if bx == 1:
            part[slot] = fields[0].reshape(lx, ly, lz)
        else:
            for b in range(bx):
                part[slot, 8 * b : 8 * b + 8] = fields[b].reshape(8, ly, lz)
            for b in range(bx - 1):
                both = part[slot, 8 * b + 7] + part[slot, 8 * b + 8]
                part[slot, 8 * b + 7] = both
                part[slot, 8 * b + 8] = both
        ysend[slot, 0] = part[slot, :, 0, :]
        ysend[slot, 1] = part[slot, :, ly - 1, :]
        packed = dot(ends, part[slot].reshape(lx * ly, lz), ((1,), (1,)))
        zsend[slot, 0] = packed[0:1]
        zsend[slot, 1] = packed[1:2]
        for o in OFFSETS:
            if exists(o):

                @pl.when(neighbour(o)[1])
                def _():
                    sending(o, slot).start()

    zlane = lax.broadcasted_iota(jnp.int32, (1, lx * ly), 1)

    def finish(slot):
        for o in OFFSETS:
            if exists(o):

                @pl.when(neighbour(o)[1])
                def _():
                    receiving(o, slot).wait()

        span = lx * ly
        gathered = []
        for side in range(2):
            by_y = []
            for cy in range(3):
                acc = zrecv[slot, side, cy, 1]
                if nx > 1:
                    low = pltpu.roll(zrecv[slot, side, cy, 0], ly, 1)
                    high = pltpu.roll(zrecv[slot, side, cy, 2], span - ly, 1)
                    acc = acc + jnp.where(zlane < ly, low, 0.0)
                    acc = acc + jnp.where(zlane >= span - ly, high, 0.0)
                by_y.append(acc)
            acc = by_y[1]
            acc = acc + jnp.where(zlane % ly == 0, pltpu.roll(by_y[0], span - (ly - 1), 1), 0.0)
            acc = acc + jnp.where(zlane % ly == ly - 1, pltpu.roll(by_y[2], ly - 1, 1), 0.0)
            gathered.append(acc)
        stacked = jnp.concatenate(gathered + [jnp.zeros((6, span), F32)], axis=0)
        spread = dot(stacked, ends, ((0,), (0,)))
        part[slot] = part[slot] + spread.reshape(lx, ly, lz)
        part[slot, 0] = part[slot, 0] + xrecv[slot, 0]
        part[slot, lx - 1] = part[slot, lx - 1] + xrecv[slot, 1]
        for side, at in ((0, 0), (1, ly - 1)):
            part[slot, :, at, :] = part[slot, :, at, :] + yrecv[slot, side, 1]
            part[slot, 0, at : at + 1, :] = (
                part[slot, 0, at : at + 1, :] + yrecv[slot, side, 0, lx - 1 : lx, :]
            )
            part[slot, lx - 1, at : at + 1, :] = (
                part[slot, lx - 1, at : at + 1, :] + yrecv[slot, side, 2, 0:1, :]
            )

    def gather_begin(slot):
        place[slot, me] = csend[slot]

        def send(n, carry):
            pltpu.make_async_remote_copy(
                src_ref=csend.at[slot],
                dst_ref=place.at[slot, me],
                send_sem=gsend_sem.at[slot],
                recv_sem=grecv_sem.at[slot],
                device_id=coords(lax.rem(me + n, devices)),
                device_id_type=MESH,
            ).start()
            return carry

        lax.fori_loop(1, devices, send, 0)

    def gather_finish(slot):
        most = place.at[slot, pl.ds(0, devices - 1)]
        pltpu.make_async_copy(most, most, gsend_sem.at[slot]).wait()
        pltpu.make_async_copy(most, most, grecv_sem.at[slot]).wait()
        for gx in range(nx):
            for gy in range(ny):
                tile = place[slot, (gx * ny + gy) * nz]
                for gz_ in range(1, nz):
                    tile = tile + place[slot, (gx * ny + gy) * nz + gz_]
                for ex in range(bx):
                    cgrid[gx * bx + ex, gy * by : gy * by + by, :] = tile[ex * by : ex * by + by]
        return cgrid[...]

    first = PITERS
    csend[first] = jnp.zeros((8, 128), F32)
    for ex in range(bx):
        csend[first, ex * by : ex * by + by, 0:bz] = off_ref[ex]
    shift = jnp.where(
        lax.broadcasted_iota(jnp.int32, (128, 128), 0) + iz * bz
        == lax.broadcasted_iota(jnp.int32, (128, 128), 1),
        1.0,
        0.0,
    ).astype(F32)
    keep = lax.broadcasted_iota(jnp.int32, (8, 128), 1) < bz
    csend[first] = dot(jnp.where(keep, csend[first], 0.0), shift)

    fields = []
    for b in range(bx):
        t = block(temp_ref, b)
        w = block(weight, b)
        wk = w * block(cond_ref, b)
        tx, ty, tz = along_x(t, derivs), dot(ky_ref[0], t), dot(t, gz_t)
        advect = block(flow_ref, b, 0) * tx + block(flow_ref, b, 1) * ty
        advect = advect + block(flow_ref, b, 2) * tz
        diffuse = along_x(wk * tx, derivs.T) + dot(ky_ref[1], wk * ty) + dot(wk * tz, gz)
        fields.append(assemble_block(-(w * advect) - diffuse))

    pl.semaphore_wait(barrier, devices - 1)
    begin(0, fields)
    gather_begin(first)
    fields = []
    squares = (derivs * derivs).T
    for b in range(bx):
        c = block(coef, b)
        jac = along_x(c, squares) + dot(ky_ref[2], c) + dot(c, gz_sq) + HELM_SHIFT * block(weight, b)
        fields.append(assemble_block(jac))
    begin(1, fields)

    def half_if(node_id, count):
        local = node_id % 8
        shared = ((local == 0) & (node_id > 0)) | ((local == 7) & (node_id < count - 1))
        return jnp.where(shared, 0.5, 1.0)

    yz_share = half_if(lax.broadcasted_iota(jnp.int32, (ly, lz), 0) + iy * ly, ny * ly)
    yz_share = yz_share * half_if(lax.broadcasted_iota(jnp.int32, (ly, lz), 1) + iz * lz, nz * lz)
    yz_share = yz_share / wyz_ref[...] * CLOCK_STEP_SIZE

    finish(0)
    for x in range(lx):
        x_share = half_if(jnp.full((ly, lz), x, jnp.int32) + ix * lx, nx * lx)
        scale = yz_share * (x_share * float(1.0 / weights[x % 8]))
        newt_ref[x] = temp_ref[x] + part[0, x] * scale

    fields = []
    for b in range(bx):
        w = block(weight, b)
        out = along_x(w * block(flow_ref, b, 0), derivs.T)
        out = out + dot(ky_ref[1], w * block(flow_ref, b, 1))
        out = out + dot(w * (block(flow_ref, b, 2) + block(newt_ref, b)), gz)
        fields.append(assemble_block(out))
    begin(2, fields)
    finish(1)
    q[...] = 1.0 / part[1]
    shift_c = 6.0 + gather_finish(first)
    padded[...] = jnp.zeros(padded.shape, F32)
    finish(2)
    resid_ref[...] = part[2]
    start, steps = fine_coefficients()
    direc[...] = resid_ref[...] * q[...] * start
    press_ref[...] = direc[...]

    cs = (grid_x, grid_y, 128)
    cinv = 1.0 / shift_c
    cl = lax.broadcasted_iota(jnp.int32, cs, 2)
    c_up = cl < grid_z - 1
    c_down = (cl > 0) & (cl < grid_z)

    def coarse_apply(v):
        padded[1 : grid_x + 1, 8 : 8 + grid_y, :] = v
        beside = padded[0:grid_x, 8 : 8 + grid_y, :] + padded[2 : grid_x + 2, 8 : 8 + grid_y, :]
        beside = beside + padded[1 : grid_x + 1, 7 : 7 + grid_y, :]
        beside = beside + padded[1 : grid_x + 1, 9 : 9 + grid_y, :]
        beside = beside + jnp.where(c_up, pltpu.roll(v, 127, 2), 0.0)
        beside = beside + jnp.where(c_down, pltpu.roll(v, 1, 2), 0.0)
        return shift_c * v - beside

    def coarse_solve(r):
        centre = 0.5 * (COARSE_HIGH + COARSE_LOW)
        half = 0.5 * (COARSE_HIGH - COARSE_LOW)
        ratio = centre / half
        rho = 1.0 / ratio
        d = r * cinv * (1.0 / centre)
        sol = d
        for _ in range(1, CHEB_C):
            r = r - coarse_apply(d)
            new = 1.0 / (2.0 * ratio - rho)
            d = (new * rho) * d + (2.0 * new / half) * (r * cinv)
            sol = sol + d
            rho = new
        return sol

    cycle = SMOOTH + 1
    total = PITERS * cycle

    def step(t, carry):
        k = lax.rem(t, cycle)
        slot = lax.rem(t, 2)
        made = []
        for b in range(bx):
            v = block(direc, b)
            c = block(coef, b)
            out = along_x(c * along_x(v, derivs), derivs.T)
            out = out + dot(ky_ref[1], c * dot(ky_ref[0], v))
            out = out + dot(c * dot(v, gz_t), gz)
            made.append(assemble_block(out + HELM_SHIFT * block(weight, b) * v))
        begin(slot, made)
        finish(slot)
        resid_ref[...] = resid_ref[...] - part[slot]

        @pl.when(k == SMOOTH - 1)
        def _():
            turn = lax.div(t, cycle)
            csend[turn] = dot(
                dot(wrow_ref[...], resid_ref[...].reshape(lx * ly, lz)), restr[...]
            )
            gather_begin(turn)
            sol = coarse_solve(gather_finish(turn))
            spread = dot(sol.reshape(grid_x * grid_y, 128), pz[...])
            direc[...] = dot(pxy[...], spread).reshape(lx, ly, lz)

        @pl.when(k != SMOOTH - 1)
        def _():
            alpha = jnp.float32(0.0)
            beta = jnp.float32(start)
            for n, (a, b) in enumerate(steps):
                alpha = jnp.where(k == n, jnp.float32(a), alpha)
                beta = jnp.where(k == n, jnp.float32(b), beta)
            direc[...] = alpha * direc[...] + beta * (resid_ref[...] * q[...])

        @pl.when(t < total - 1)
        def _():
            press_ref[...] = press_ref[...] + direc[...]

        return carry

    lax.fori_loop(0, total, step, 0)


def shards(sizes, temp, flow, cond, vol, off):
    derivs, weights = gll_tables()
    lx, ly, lz = temp.shape
    blocks = off.shape
    bx, by, bz = blocks
    devices = sizes[0] * sizes[1] * sizes[2]
    squares = derivs * derivs
    eye_z = np.eye(bz, dtype=np.float32)
    eye_y = np.eye(ly, dtype=np.float32)
    gz = np.stack([np.kron(eye_z, derivs.T), np.kron(eye_z, derivs), np.kron(eye_z, squares)])
    ky = np.stack([np.kron(eye_y, derivs), np.kron(eye_y, derivs.T), np.kron(eye_y, squares.T)])
    w_y, w_z = np.tile(weights, by), np.tile(weights, bz)
    wyz = w_y[:, None] * w_z[None, :]
    wcol = np.broadcast_to(w_z[:, None], (lz, 128))
    wrow = np.zeros((8, lx * ly), np.float32)
    for ex in range(bx):
        for ey in range(by):
            for a in range(8):
                at = (ex * 8 + a) * ly + ey * 8
                wrow[ex * by + ey, at : at + 8] = weights[a] * weights
    cube = jax.ShapeDtypeStruct((lx, ly, lz), jnp.float32)
    vmem = pl.BlockSpec(memory_space=pltpu.VMEM)
    grid = (sizes[0] * bx, sizes[1] * by)
    scratch = [
        pltpu.VMEM((lx, ly, lz), F32),
        pltpu.VMEM((lx, ly, lz), F32),
        pltpu.VMEM((lx, ly, lz), F32),
        pltpu.VMEM((lx, ly, lz), F32),
        pltpu.VMEM((3, lx, ly, lz), F32),
        pltpu.VMEM((3, 2, lx, lz), F32),
        pltpu.VMEM((3, 2, 1, lx * ly), F32),
        pltpu.VMEM((3, 2, ly, lz), F32),
        pltpu.VMEM((3, 2, 3, lx, lz), F32),
        pltpu.VMEM((3, 2, 3, 3, 1, lx * ly), F32),
        pltpu.VMEM((PITERS + 1, devices, 8, 128), F32),
        pltpu.VMEM((PITERS + 1, 8, 128), F32),
        pltpu.VMEM((grid[0], grid[1], 128), F32),
        pltpu.VMEM((grid[0] + 2, grid[1] + 16, 128), F32),
        pltpu.VMEM((128, lz), F32),
        pltpu.VMEM((lx * ly, grid[0] * grid[1]), F32),
        pltpu.VMEM((lz, 128), F32),
        pltpu.SemaphoreType.DMA((3, len(OFFSETS))),
        pltpu.SemaphoreType.DMA((3, len(OFFSETS))),
        pltpu.SemaphoreType.DMA((PITERS + 1,)),
        pltpu.SemaphoreType.DMA((PITERS + 1,)),
    ]
    return pl.pallas_call(
        functools.partial(kernel, sizes, blocks),
        out_shape=(cube, cube, cube),
        in_specs=[vmem] * 10,
        out_specs=(vmem, vmem, vmem),
        scratch_shapes=scratch,
        compiler_params=pltpu.CompilerParams(
            collective_id=0, has_side_effects=True, vmem_limit_bytes=40 * 1024 * 1024
        ),
        name="spectral_step",
    )(temp, flow, cond, vol, off, gz, ky, wyz, wcol, wrow)


def solution(mesh):
    cube = P("gx", "gy", "gz")
    sizes = tuple(mesh.shape[name] for name in ("gx", "gy", "gz"))
    return jax.shard_map(
        functools.partial(shards, sizes),
        mesh=mesh,
        in_specs=(cube, P(None, "gx", "gy", "gz"), cube, cube, cube),
        out_specs=(cube, cube, cube),
        check_vma=False,
    )
```

time: 837 us -> 93.5 us (0.11); the launches traced: 823 us -> 93.2 us
  starting transfers between devices: 337 us -> 0 us
  waiting for transfers between devices: 334 us -> 0 us
  Pallas kernels: 0 us -> 83.6 us
  matrix products: 47.1 us -> 0 us
  other arithmetic: 45.3 us -> 0 us
  local copies, waits for them, and re-layouts: 54.2 us -> 8.91 us
    ppermute x168 -> x0, starting transfers between devices: 337 us -> none  [the longest x84 228 us: extended(): lax.ppermute(tail, axis, [(i, (i + 1) % count) for i in range(ends)])]
    ppermute x168 -> x0, waiting for transfers between devices: 334 us -> none  [the longest x84 238 us: extended(): lax.ppermute(head, axis, [((i + 1) % count, i) for i in range(ends)])]
    pallas_call x0 -> x1, Pallas kernels: none -> 83.6 us  [shards(): pl.pallas_call(functools.partial(kernel, sizes, blocks), out_shape=(cube,...]
    dot_general x62 -> x0, matrix products: 47.1 us -> none  [the longest x20 18.8 us: apply_derivative_matrix(): jnp.dot(values.reshape(length_along_x * length_along_y, length_along_z),...]
    add x42 -> x0, other arithmetic: 17.9 us -> none  [the longest x25 13.9 us: pair_pass(): padded + jnp.where(position == 0, shifted_up, 0.0)]
    another operation x9 -> x1, local copies, waits for them, and re-layouts: 17 us -> 0.74 us  [the longest x8 13.4 us: shards(): quadrature_coefficient = jnp.tile(cube_w, (blocks_x, blocks_y, blocks_z))]
    slice x100 -> x0, local copies, waits for them, and re-layouts: 13.5 us -> none  [the longest x41 6.39 us: pair_pass(): lax.slice_in_dim(padded, 1, extent, axis=direction_index)]
    sub x14 -> x0, other arithmetic: 12.2 us -> none  [the longest x9 8.4 us: chebyshev(): equation_misfit = equation_misfit - apply_fn(direction)]
  transfers between devices with their start and end apart: 168 -> 0, of which waited for: 99 -> 0; matrix products, arithmetic and copies ran while one was open for 4% -> 0% of each run, Pallas kernels for 0% -> 0%
where the time goes in v1:
time: 93.5 us; the launch traced here: 93.2 us
  Pallas kernels  83.6 us (89%)
  local copies, waits for them, and re-layouts  8.91 us (10%)
    pallas_call x1, Pallas kernels, shards(): pl.pallas_call(functools.partial(kernel, sizes, blocks), out_shape=(cube,...  83.6 us
    unnamed x21, local copies, waits for them, and re-layouts  8.16 us

profile of v1, /device:TPU:0, one launch (start us, length us, event | category | flops | bytes accessed | tf_op | source)
XLA Modules:
  0.0 93.2 jit_solution(3695358363838527016)
XLA Ops:
  0.6 0.0 copy-start.6
  0.6 0.0 copy-start.7
  0.7 0.0 copy-start.8
  0.7 0.7 jit_solution_.3.wcol_ref
  1.4 0.0 copy-done.6
  1.4 0.0 copy-done.7
  1.4 0.0 copy-done.8
  1.4 0.0 copy-start
  1.4 1.1 %copy-done = f32[3,16,32,128]{3,2,1,0:T(8,128)S(1)} copy-done((f32[3,16,32,128]{3,2,1,0:T(8,128)S(1)}, f32[3,16,32,128]{3,2,1,0:T(8,128)}, u32[]{:S(2)}) %copy-start) | copy-done | bytes 786456
  2.6 0.0 copy-start.1
  2.6 1.1 %copy-done.1 = f32[3,256,256]{2,1,0:T(8,128)S(1)} copy-done((f32[3,256,256]{2,1,0:T(8,128)S(1)}, f32[3,256,256]{2,1,0:T(8,128)}, u32[]{:S(2)}) %copy-start.1) | copy-done | bytes 786456
  3.7 0.0 copy-start.2
  3.7 0.9 %copy-done.2 = f32[16,32,128]{2,1,0:T(8,128)S(1)} copy-done((f32[16,32,128]{2,1,0:T(8,128)S(1)}, f32[16,32,128]{2,1,0:T(8,128)}, u32[]{:S(2)}) %copy-start.2) | copy-done | bytes 262168
  4.7 0.0 copy-start.3
  4.7 0.9 %copy-done.3 = f32[16,32,128]{2,1,0:T(8,128)S(1)} copy-done((f32[16,32,128]{2,1,0:T(8,128)S(1)}, f32[16,32,128]{2,1,0:T(8,128)}, u32[]{:S(2)}) %copy-start.3) | copy-done | bytes 262168
  5.6 0.0 copy-start.4
  5.6 0.9 %copy-done.4 = f32[16,32,128]{2,1,0:T(8,128)S(1)} copy-done((f32[16,32,128]{2,1,0:T(8,128)S(1)}, f32[16,32,128]{2,1,0:T(8,128)}, u32[]{:S(2)}) %copy-start.4) | copy-done | bytes 262168
  6.6 0.0 copy-start.5
  6.6 0.9 copy-done.5
  7.5 83.6 %spectral_step.1 = (f32[16,32,128]{2,1,0:T(8,128)S(1)}, f32[16,32,128]{2,1,0:T(8,128)S(1)}, f32[16,32,128]{2,1,0:T(8,128)S(1)}) custom-call(f32[16,32,128]{2,1,0:T(8,128)S(1)} %copy-done.2, f32[3,16,32,128]{3,2,1,0:T(8,128)S(1)} %copy-done, f32[16,32,128]{2,1,0:T(8,128)S(1)} %copy-done.3, f32[16,32,128]{2,1,0:T(8,128)S(1)} %copy-done.4, ...), custom_call_target="tpu_custom_call" | custom-call | tf_op jit(solution)/shard_map/spectral_step/pallas_call | solution.py:553
  91.1 0.7 copy.16
  91.8 0.7 copy.17
  92.5 0.7 copy.18
Async XLA Ops:
  0.6 0.8 copy-start.6
  0.6 0.8 copy-start.7
  0.7 0.8 copy-start.8
  1.4 1.1 %copy-start = (f32[3,16,32,128]{3,2,1,0:T(8,128)S(1)}, f32[3,16,32,128]{3,2,1,0:T(8,128)}, u32[]{:S(2)}) copy-start(f32[3,16,32,128]{3,2,1,0:T(8,128)} %flow_ref.1) | copy-start | bytes 2359300
  2.6 1.1 %copy-start.1 = (f32[3,256,256]{2,1,0:T(8,128)S(1)}, f32[3,256,256]{2,1,0:T(8,128)}, u32[]{:S(2)}) copy-start(f32[3,256,256]{2,1,0:T(8,128)} %constant.11.clone.ky_ref) | copy-start | bytes 2359300
  3.7 0.9 %copy-start.2 = (f32[16,32,128]{2,1,0:T(8,128)S(1)}, f32[16,32,128]{2,1,0:T(8,128)}, u32[]{:S(2)}) copy-start(f32[16,32,128]{2,1,0:T(8,128)} %temp_ref.1) | copy-start | bytes 786436
  4.7 0.9 %copy-start.3 = (f32[16,32,128]{2,1,0:T(8,128)S(1)}, f32[16,32,128]{2,1,0:T(8,128)}, u32[]{:S(2)}) copy-start(f32[16,32,128]{2,1,0:T(8,128)} %cond_ref.1) | copy-start | bytes 786436
  5.6 0.9 %copy-start.4 = (f32[16,32,128]{2,1,0:T(8,128)S(1)}, f32[16,32,128]{2,1,0:T(8,128)}, u32[]{:S(2)}) copy-start(f32[16,32,128]{2,1,0:T(8,128)} %vol_ref.1) | copy-start | bytes 786436
  6.6 0.9 copy-start.5

commit v2 on v1

--- a/solution.py
+++ b/solution.py
@@ -63,6 +63,45 @@
     return lax.dot_general(a, b, (dims, ((), ())), precision=HIGHEST, preferred_element_type=F32)
 
 
+BF16 = jnp.bfloat16
+
+
+def narrow(v, terms):
+    out = []
+    for n in range(terms):
+        piece = v.astype(BF16)
+        out.append(piece)
+        if n < terms - 1:
+            v = v - piece.astype(F32)
+    return out
+
+
+def bdot(a, b, dims=((1,), (0,))):
+    return lax.dot_general(a, b, (dims, ((), ())), preferred_element_type=F32)
+
+
+def right(v, pair):
+    width = v.shape[1]
+    out = bdot(jnp.concatenate(narrow(v, 2), axis=1), pair)
+    return out[:, :width] + out[:, width:]
+
+
+def left(high, low, v):
+    width = v.shape[1]
+    pieces = narrow(v, 2)
+    out = bdot(high, jnp.concatenate(pieces, axis=1))
+    return out[:, :width] + out[:, width:] + bdot(low, pieces[0])
+
+
+def reach(sizes, blocks):
+    out = []
+    for o in itertools.product(*(range(1 - s, s) for s in sizes)):
+        far = sum(max(abs(d) - 1, 0) * b for d, b in zip(o, blocks))
+        if far < CHEB_C and o != (0, 0, 0):
+            out.append(o)
+    return out
+
+
 def fine_coefficients():
     centre = 0.5 * (FINE_HIGH + FINE_LOW)
     half = 0.5 * (FINE_HIGH - FINE_LOW)
@@ -79,19 +118,21 @@
 def kernel(
     sizes,
     blocks,
+    temp_hbm,
+    flow_hbm,
+    cond_hbm,
+    vol_hbm,
+    off_ref,
+    mats_ref,
+    rows_ref,
+    newt_ref,
+    press_ref,
+    resid_ref,
     temp_ref,
     flow_ref,
     cond_ref,
     vol_ref,
-    off_ref,
-    gz_ref,
-    ky_ref,
-    wyz_ref,
-    wcol_ref,
-    wrow_ref,
-    newt_ref,
-    press_ref,
-    resid_ref,
+    in_sem,
     weight,
     coef,
     q,
@@ -104,11 +145,11 @@
     zrecv,
     place,
     csend,
+    ctile,
     cgrid,
     padded,
     pz,
     pxy,
-    restr,
     send_sem,
     recv_sem,
     gsend_sem,
@@ -124,22 +165,45 @@
     ix, iy, iz = lax.axis_index("gx"), lax.axis_index("gy"), lax.axis_index("gz")
     me = (ix * ny + iy) * nz + iz
 
-    def coords(linear):
-        return (linear // (ny * nz), (linear // nz) % ny, linear % nz)
+    loads = [
+        pltpu.make_async_copy(a, b, in_sem.at[n])
+        for n, (a, b) in enumerate(
+            (
+                (temp_hbm, temp_ref),
+                (flow_hbm, flow_ref),
+                (cond_hbm, cond_ref),
+                (vol_hbm, vol_ref),
+            )
+        )
+    ]
+    for load in loads:
+        load.start()
 
     xrecv[...] = jnp.zeros(xrecv.shape, F32)
     yrecv[...] = jnp.zeros(yrecv.shape, F32)
     zrecv[...] = jnp.zeros(zrecv.shape, F32)
+    place[...] = jnp.zeros(place.shape, F32)
+    partners = reach(sizes, blocks)
+
+    def neighbour(o):
+        to = (ix + o[0], iy + o[1], iz + o[2])
+        there = None
+        for value, size, step in zip(to, sizes, o):
+            if step:
+                ok = (value >= 0) if step < 0 else (value < size)
+                there = ok if there is None else (there & ok)
+        return to, there
 
     barrier = pltpu.get_barrier_semaphore()
 
-    def greet(n, carry):
-        pl.semaphore_signal(
-            barrier, inc=1, device_id=coords(lax.rem(me + n, devices)), device_id_type=MESH
-        )
-        return carry
-
-    lax.fori_loop(1, devices, greet, 0)
+    met = jnp.int32(0)
+    for o in partners:
+        to, there = neighbour(o)
+        met = met + jnp.where(there, 1, 0)
+
+        @pl.when(there)
+        def _():
+            pl.semaphore_signal(barrier, inc=1, device_id=to, device_id_type=MESH)
 
     lane = lax.broadcasted_iota(jnp.int32, (rows, lz), 1)
     row_y = lax.broadcasted_iota(jnp.int32, (rows, lz), 0) % ly
@@ -148,9 +212,9 @@
     y_up = (row_y % 8 == 7) & (row_y < ly - 1)
     y_down = (row_y % 8 == 0) & (row_y > 0)
 
+    wyz = rows_ref[0:ly]
     for x in range(lx):
-        weight[x] = wyz_ref[...] * float(weights[x % 8])
-    coef[...] = weight[...] * vol_ref[...]
+        weight[x] = wyz * float(weights[x % 8])
 
     def share(node, elements, element):
         owner = node // 8
@@ -165,18 +229,25 @@
         lax.broadcasted_iota(jnp.int32, (128, lz), 1) + iz * lz,
         grid_z,
         lax.broadcasted_iota(jnp.int32, (128, lz), 0),
-    )
+    ).astype(BF16)
     node = lax.broadcasted_iota(jnp.int32, (lx * ly, grid_x * grid_y), 0)
     elem = lax.broadcasted_iota(jnp.int32, (lx * ly, grid_x * grid_y), 1)
-    pxy[...] = share(node // ly + ix * lx, grid_x, elem // grid_y) * share(
-        node % ly + iy * ly, grid_y, elem % grid_y
-    )
-    here = lax.broadcasted_iota(jnp.int32, (lz, 128), 0) // 8 + iz * bz
-    restr[...] = jnp.where(
-        here == lax.broadcasted_iota(jnp.int32, (lz, 128), 1), wcol_ref[...] * 0.125, 0.0
-    )
-
-    gz_t, gz, gz_sq = gz_ref[0], gz_ref[1], gz_ref[2]
+    pxy[...] = (
+        share(node // ly + ix * lx, grid_x, elem // grid_y)
+        * share(node % ly + iy * ly, grid_y, elem % grid_y)
+    ).astype(BF16)
+    restr = rows_ref[ly : ly + 128]
+    spot = lax.broadcasted_iota(jnp.int32, (8, 128), 1)
+    own_row = spot // bz == lax.broadcasted_iota(jnp.int32, (8, 128), 0)
+    from_lane = lax.broadcasted_iota(jnp.int32, (128, 128), 0)
+    to_lane = lax.broadcasted_iota(jnp.int32, (128, 128), 1)
+    fold = jnp.where(from_lane % bz == to_lane % bz, 1.0, 0.0).astype(BF16)
+
+    def along_z(v, n):
+        return right(v, mats_ref[n])
+
+    def along_y(v, n):
+        return left(mats_ref[3 + n], mats_ref[6 + n], v)
 
     def along_x(v, matrix):
         layers = [v[a * ly : (a + 1) * ly] for a in range(8)]
@@ -205,23 +276,12 @@
             + jnp.where(y_down, pltpu.roll(v, 1, 0), 0.0)
         )
 
-    ends = (lax.broadcasted_iota(jnp.int32, (8, lz), 0) == 0) & (
-        lax.broadcasted_iota(jnp.int32, (8, lz), 1) == 0
-    )
-    ends = ends | (
-        (lax.broadcasted_iota(jnp.int32, (8, lz), 0) == 1)
-        & (lax.broadcasted_iota(jnp.int32, (8, lz), 1) == lz - 1)
-    )
-    ends = jnp.where(ends, 1.0, 0.0).astype(F32)
-
-    def neighbour(o):
-        to = (ix + o[0], iy + o[1], iz + o[2])
-        there = None
-        for value, size, step in zip(to, sizes, o):
-            if step:
-                ok = (value >= 0) if step < 0 else (value < size)
-                there = ok if there is None else (there & ok)
-        return to, there
+    end_row = lax.broadcasted_iota(jnp.int32, (16, lz), 0)
+    end_lane = lax.broadcasted_iota(jnp.int32, (16, lz), 1)
+    ends = jnp.where(
+        (end_row < 6) & (end_lane == jnp.where(end_row % 2 == 0, 0, lz - 1)), 1.0, 0.0
+    ).astype(BF16)
+    ends_three = jnp.concatenate([ends] * 3, axis=1)
 
     def buffers(o, slot):
         ox, oy, oz = o
@@ -280,7 +340,8 @@
                 part[slot, 8 * b + 8] = both
         ysend[slot, 0] = part[slot, :, 0, :]
         ysend[slot, 1] = part[slot, :, ly - 1, :]
-        packed = dot(ends, part[slot].reshape(lx * ly, lz), ((1,), (1,)))
+        whole = jnp.concatenate(narrow(part[slot].reshape(lx * ly, lz), 3), axis=1)
+        packed = bdot(ends_three, whole, ((1,), (1,)))
         zsend[slot, 0] = packed[0:1]
         zsend[slot, 1] = packed[1:2]
         for o in OFFSETS:
@@ -316,8 +377,9 @@
             acc = acc + jnp.where(zlane % ly == 0, pltpu.roll(by_y[0], span - (ly - 1), 1), 0.0)
             acc = acc + jnp.where(zlane % ly == ly - 1, pltpu.roll(by_y[2], ly - 1, 1), 0.0)
             gathered.append(acc)
-        stacked = jnp.concatenate(gathered + [jnp.zeros((6, span), F32)], axis=0)
-        spread = dot(stacked, ends, ((0,), (0,)))
+        pieces = [p.astype(F32) for p in narrow(jnp.concatenate(gathered, axis=0), 3)]
+        stacked = jnp.concatenate(pieces + [jnp.zeros((10, span), F32)], axis=0)
+        spread = bdot(stacked.astype(BF16), ends, ((0,), (0,)))
         part[slot] = part[slot] + spread.reshape(lx, ly, lz)
         part[slot, 0] = part[slot, 0] + xrecv[slot, 0]
         part[slot, lx - 1] = part[slot, lx - 1] + xrecv[slot, 1]
@@ -330,67 +392,83 @@
                 part[slot, lx - 1, at : at + 1, :] + yrecv[slot, side, 2, 0:1, :]
             )
 
-    def gather_begin(slot):
+    def gather_begin(slot, tile):
+        csend[slot] = jnp.sum(jnp.where(own_row, tile, 0.0), axis=0, keepdims=True)
         place[slot, me] = csend[slot]
-
-        def send(n, carry):
-            pltpu.make_async_remote_copy(
-                src_ref=csend.at[slot],
-                dst_ref=place.at[slot, me],
-                send_sem=gsend_sem.at[slot],
-                recv_sem=grecv_sem.at[slot],
-                device_id=coords(lax.rem(me + n, devices)),
-                device_id_type=MESH,
-            ).start()
-            return carry
-
-        lax.fori_loop(1, devices, send, 0)
+        for o in partners:
+            to, there = neighbour(o)
+
+            @pl.when(there)
+            def _():
+                gather_copy(slot, o).start()
+
+    def gather_copy(slot, o, arriving=False):
+        to, _ = neighbour(o)
+        other = (to[0] * ny + to[1]) * nz + to[2]
+        return pltpu.make_async_remote_copy(
+            src_ref=csend.at[slot],
+            dst_ref=place.at[slot, other if arriving else me],
+            send_sem=gsend_sem.at[slot, partners.index(o)],
+            recv_sem=grecv_sem.at[slot, partners.index(tuple(d if arriving else -d for d in o))],
+            device_id=to,
+            device_id_type=MESH,
+        )
 
     def gather_finish(slot):
-        most = place.at[slot, pl.ds(0, devices - 1)]
-        pltpu.make_async_copy(most, most, gsend_sem.at[slot]).wait()
-        pltpu.make_async_copy(most, most, grecv_sem.at[slot]).wait()
+        for o in partners:
+            to, there = neighbour(o)
+
+            @pl.when(there)
+            def _():
+                gather_copy(slot, o, True).wait()
+
+        shape = (devices, 8, 128)
+        box_lane = lax.broadcasted_iota(jnp.int32, shape, 2) // bz
+        box_row = lax.broadcasted_iota(jnp.int32, shape, 1)
+        box_z = lax.broadcasted_iota(jnp.int32, shape, 0) % nz
+        boxes = jnp.where(box_lane == box_row, jnp.broadcast_to(place[slot], shape), 0.0)
+        boxes = boxes.reshape(devices * 8, 128)
+        moved = bdot(jnp.concatenate(narrow(boxes, 3), axis=1), jnp.concatenate([fold] * 3, axis=0))
+        moved = jnp.where(box_lane == box_z, moved.reshape(shape), 0.0)
         for gx in range(nx):
             for gy in range(ny):
-                tile = place[slot, (gx * ny + gy) * nz]
-                for gz_ in range(1, nz):
-                    tile = tile + place[slot, (gx * ny + gy) * nz + gz_]
+                at = (gx * ny + gy) * nz
+                tile = moved[at]
+                for gz in range(1, nz):
+                    tile = tile + moved[at + gz]
                 for ex in range(bx):
                     cgrid[gx * bx + ex, gy * by : gy * by + by, :] = tile[ex * by : ex * by + by]
         return cgrid[...]
 
     first = PITERS
-    csend[first] = jnp.zeros((8, 128), F32)
+    ctile[...] = jnp.zeros((8, 128), F32)
     for ex in range(bx):
-        csend[first, ex * by : ex * by + by, 0:bz] = off_ref[ex]
-    shift = jnp.where(
-        lax.broadcasted_iota(jnp.int32, (128, 128), 0) + iz * bz
-        == lax.broadcasted_iota(jnp.int32, (128, 128), 1),
-        1.0,
-        0.0,
-    ).astype(F32)
-    keep = lax.broadcasted_iota(jnp.int32, (8, 128), 1) < bz
-    csend[first] = dot(jnp.where(keep, csend[first], 0.0), shift)
+        ctile[ex * by : ex * by + by, 0:bz] = off_ref[ex]
+    spread_out = jnp.where((from_lane < bz) & (from_lane == to_lane % bz), 1.0, 0.0).astype(F32)
+    off_tile = dot(ctile[...], spread_out)
+    for load in loads:
+        load.wait()
+    coef[...] = weight[...] * vol_ref[...]
 
     fields = []
     for b in range(bx):
         t = block(temp_ref, b)
         w = block(weight, b)
         wk = w * block(cond_ref, b)
-        tx, ty, tz = along_x(t, derivs), dot(ky_ref[0], t), dot(t, gz_t)
+        tx, ty, tz = along_x(t, derivs), along_y(t, 0), along_z(t, 0)
         advect = block(flow_ref, b, 0) * tx + block(flow_ref, b, 1) * ty
         advect = advect + block(flow_ref, b, 2) * tz
-        diffuse = along_x(wk * tx, derivs.T) + dot(ky_ref[1], wk * ty) + dot(wk * tz, gz)
+        diffuse = along_x(wk * tx, derivs.T) + along_y(wk * ty, 1) + along_z(wk * tz, 1)
         fields.append(assemble_block(-(w * advect) - diffuse))
 
-    pl.semaphore_wait(barrier, devices - 1)
+    pl.semaphore_wait(barrier, met)
     begin(0, fields)
-    gather_begin(first)
+    gather_begin(first, off_tile)
     fields = []
     squares = (derivs * derivs).T
     for b in range(bx):
         c = block(coef, b)
-        jac = along_x(c, squares) + dot(ky_ref[2], c) + dot(c, gz_sq) + HELM_SHIFT * block(weight, b)
+        jac = along_x(c, squares) + along_y(c, 2) + along_z(c, 2) + HELM_SHIFT * block(weight, b)
         fields.append(assemble_block(jac))
     begin(1, fields)
 
@@ -401,7 +479,7 @@
 
     yz_share = half_if(lax.broadcasted_iota(jnp.int32, (ly, lz), 0) + iy * ly, ny * ly)
     yz_share = yz_share * half_if(lax.broadcasted_iota(jnp.int32, (ly, lz), 1) + iz * lz, nz * lz)
-    yz_share = yz_share / wyz_ref[...] * CLOCK_STEP_SIZE
+    yz_share = yz_share / wyz * CLOCK_STEP_SIZE
 
     finish(0)
     for x in range(lx):
@@ -413,8 +491,8 @@
     for b in range(bx):
         w = block(weight, b)
         out = along_x(w * block(flow_ref, b, 0), derivs.T)
-        out = out + dot(ky_ref[1], w * block(flow_ref, b, 1))
-        out = out + dot(w * (block(flow_ref, b, 2) + block(newt_ref, b)), gz)
+        out = out + along_y(w * block(flow_ref, b, 1), 1)
+        out = out + along_z(w * (block(flow_ref, b, 2) + block(newt_ref, b)), 1)
         fields.append(assemble_block(out))
     begin(2, fields)
     finish(1)
@@ -468,8 +546,8 @@
             v = block(direc, b)
             c = block(coef, b)
             out = along_x(c * along_x(v, derivs), derivs.T)
-            out = out + dot(ky_ref[1], c * dot(ky_ref[0], v))
-            out = out + dot(c * dot(v, gz_t), gz)
+            out = out + along_y(c * along_y(v, 0), 1)
+            out = out + along_z(c * along_z(v, 0), 1)
             made.append(assemble_block(out + HELM_SHIFT * block(weight, b) * v))
         begin(slot, made)
         finish(slot)
@@ -478,13 +556,21 @@
         @pl.when(k == SMOOTH - 1)
         def _():
             turn = lax.div(t, cycle)
-            csend[turn] = dot(
-                dot(wrow_ref[...], resid_ref[...].reshape(lx * ly, lz)), restr[...]
-            )
-            gather_begin(turn)
-            sol = coarse_solve(gather_finish(turn))
-            spread = dot(sol.reshape(grid_x * grid_y, 128), pz[...])
-            direc[...] = dot(pxy[...], spread).reshape(lx, ly, lz)
+            sums = []
+            for b in range(bx):
+                acc = resid_ref[8 * b] * float(weights[0])
+                for a in range(1, 8):
+                    acc = acc + resid_ref[8 * b + a] * float(weights[a])
+                sums.append(acc * rows_ref[ly + 128 : 2 * ly + 128])
+            sums = dot(jnp.concatenate(sums, axis=0), restr)
+            gather_begin(turn, jnp.sum(sums.reshape(bx * by, 8, 128), axis=1))
+            sol = coarse_solve(gather_finish(turn)).reshape(grid_x * grid_y, 128)
+            count = grid_x * grid_y
+            along = bdot(jnp.concatenate(narrow(sol, 3), axis=0), pz[...])
+            along = along[0:count] + along[count : 2 * count] + along[2 * count :]
+            wide = bdot(pxy[...], jnp.concatenate(narrow(along, 3), axis=1))
+            wide = wide[:, 0:lz] + wide[:, lz : 2 * lz] + wide[:, 2 * lz :]
+            direc[...] = wide.reshape(lx, ly, lz)
 
         @pl.when(k != SMOOTH - 1)
         def _():
@@ -513,21 +599,35 @@
     squares = derivs * derivs
     eye_z = np.eye(bz, dtype=np.float32)
     eye_y = np.eye(ly, dtype=np.float32)
-    gz = np.stack([np.kron(eye_z, derivs.T), np.kron(eye_z, derivs), np.kron(eye_z, squares)])
-    ky = np.stack([np.kron(eye_y, derivs), np.kron(eye_y, derivs.T), np.kron(eye_y, squares.T)])
+
+    def halves(m):
+        high = m.astype(BF16)
+        return high, (m - high.astype(np.float32)).astype(BF16)
+
+    mats = np.zeros((9, 8 * ly, 8 * ly), BF16)
+    for n, m in enumerate((derivs.T, derivs, squares)):
+        high, low = halves(np.kron(eye_z, m))
+        mats[n, :lz, :lz] = high
+        mats[n, :lz, lz:] = low
+        mats[n, lz:, :lz] = high
+        mats[3 + n], mats[6 + n] = halves(np.kron(eye_y, m.T))
     w_y, w_z = np.tile(weights, by), np.tile(weights, bz)
     wyz = w_y[:, None] * w_z[None, :]
-    wcol = np.broadcast_to(w_z[:, None], (lz, 128))
-    wrow = np.zeros((8, lx * ly), np.float32)
-    for ex in range(bx):
-        for ey in range(by):
-            for a in range(8):
-                at = (ex * 8 + a) * ly + ey * 8
-                wrow[ex * by + ey, at : at + 8] = weights[a] * weights
+    lanes = np.arange(128)[None, :] % bz == np.arange(lz)[:, None] // 8
+    restr = np.where(lanes, w_z[:, None] * np.float32(0.125), np.float32(0.0))
+    wy_rows = np.broadcast_to(w_y[:, None], (ly, 128))
+    table = np.concatenate([wyz, restr, wy_rows], axis=0).astype(np.float32)
     cube = jax.ShapeDtypeStruct((lx, ly, lz), jnp.float32)
     vmem = pl.BlockSpec(memory_space=pltpu.VMEM)
     grid = (sizes[0] * bx, sizes[1] * by)
+    hbm = pl.BlockSpec(memory_space=pl.ANY)
+    span = len(reach(sizes, blocks))
     scratch = [
+        pltpu.VMEM((lx, ly, lz), F32),
+        pltpu.VMEM((3, lx, ly, lz), F32),
+        pltpu.VMEM((lx, ly, lz), F32),
+        pltpu.VMEM((lx, ly, lz), F32),
+        pltpu.SemaphoreType.DMA((4,)),
         pltpu.VMEM((lx, ly, lz), F32),
         pltpu.VMEM((lx, ly, lz), F32),
         pltpu.VMEM((lx, ly, lz), F32),
@@ -538,29 +638,29 @@
         pltpu.VMEM((3, 2, ly, lz), F32),
         pltpu.VMEM((3, 2, 3, lx, lz), F32),
         pltpu.VMEM((3, 2, 3, 3, 1, lx * ly), F32),
-        pltpu.VMEM((PITERS + 1, devices, 8, 128), F32),
-        pltpu.VMEM((PITERS + 1, 8, 128), F32),
+        pltpu.VMEM((PITERS + 1, devices, 1, 128), F32),
+        pltpu.VMEM((PITERS + 1, 1, 128), F32),
+        pltpu.VMEM((8, 128), F32),
         pltpu.VMEM((grid[0], grid[1], 128), F32),
         pltpu.VMEM((grid[0] + 2, grid[1] + 16, 128), F32),
-        pltpu.VMEM((128, lz), F32),
-        pltpu.VMEM((lx * ly, grid[0] * grid[1]), F32),
-        pltpu.VMEM((lz, 128), F32),
+        pltpu.VMEM((128, lz), BF16),
+        pltpu.VMEM((lx * ly, grid[0] * grid[1]), BF16),
         pltpu.SemaphoreType.DMA((3, len(OFFSETS))),
         pltpu.SemaphoreType.DMA((3, len(OFFSETS))),
-        pltpu.SemaphoreType.DMA((PITERS + 1,)),
-        pltpu.SemaphoreType.DMA((PITERS + 1,)),
+        pltpu.SemaphoreType.DMA((PITERS + 1, span)),
+        pltpu.SemaphoreType.DMA((PITERS + 1, span)),
     ]
     return pl.pallas_call(
         functools.partial(kernel, sizes, blocks),
         out_shape=(cube, cube, cube),
-        in_specs=[vmem] * 10,
+        in_specs=[hbm] * 4 + [vmem] * 3,
         out_specs=(vmem, vmem, vmem),
         scratch_shapes=scratch,
         compiler_params=pltpu.CompilerParams(
             collective_id=0, has_side_effects=True, vmem_limit_bytes=40 * 1024 * 1024
         ),
         name="spectral_step",
-    )(temp, flow, cond, vol, off, gz, ky, wyz, wcol, wrow)
+    )(temp, flow, cond, vol, off, jnp.asarray(mats), jnp.asarray(table))
 
 
 def solution(mesh):

time: 93.5 us -> 80.4 us (0.86)
  Pallas kernels: 83.6 us -> 70.5 us
    pallas_call x1, Pallas kernels: 83.6 us -> 70.5 us  [shards(): pl.pallas_call(functools.partial(kernel, sizes, blocks), out_shape=(cube,...]
    unnamed x21 -> x17, local copies, waits for them, and re-layouts: 8.16 us -> 8.94 us
where the time goes in v2:
time: 80.4 us; the launch traced here: 80.1 us
  Pallas kernels  70.5 us (88%)
  local copies, waits for them, and re-layouts  8.94 us (11%)
    pallas_call x1, Pallas kernels, shards(): pl.pallas_call(functools.partial(kernel, sizes, blocks), out_shape=(cube,...  70.5 us
    unnamed x17, local copies, waits for them, and re-layouts  8.94 us

profile of v2, /device:TPU:0, one launch (start us, length us, event | category | flops | bytes accessed | tf_op | source)
XLA Modules:
  0.0 80.1 jit_solution(15185891085619735389)
XLA Ops:
  0.6 0.0 copy-start
  0.6 1.3 %copy-done = bf16[9,256,256]{2,1,0:T(8,128)(2,1)S(1)} copy-done((bf16[9,256,256]{2,1,0:T(8,128)(2,1)S(1)}, bf16[9,256,256]{2,1,0:T(8,128)(2,1)}, u32[]{:S(2)}) %copy-start) | copy-done | bytes 1179672
  1.9 0.0 copy-start.1
  1.9 1.1 %copy-done.1 = f32[3,16,32,128]{3,2,1,0:T(8,128)S(1)} copy-done((f32[3,16,32,128]{3,2,1,0:T(8,128)S(1)}, f32[3,16,32,128]{3,2,1,0:T(8,128)}, u32[]{:S(2)}) %copy-start.1) | copy-done | bytes 786456
  3.0 0.0 copy-start.2
  3.0 0.9 %copy-done.2 = f32[16,32,128]{2,1,0:T(8,128)S(1)} copy-done((f32[16,32,128]{2,1,0:T(8,128)S(1)}, f32[16,32,128]{2,1,0:T(8,128)}, u32[]{:S(2)}) %copy-start.2) | copy-done | bytes 262168
  4.0 0.0 copy-start.3
  4.0 0.9 %copy-done.3 = f32[16,32,128]{2,1,0:T(8,128)S(1)} copy-done((f32[16,32,128]{2,1,0:T(8,128)S(1)}, f32[16,32,128]{2,1,0:T(8,128)}, u32[]{:S(2)}) %copy-start.3) | copy-done | bytes 262168
  4.9 0.0 copy-start.4
  4.9 0.9 %copy-done.4 = f32[16,32,128]{2,1,0:T(8,128)S(1)} copy-done((f32[16,32,128]{2,1,0:T(8,128)S(1)}, f32[16,32,128]{2,1,0:T(8,128)}, u32[]{:S(2)}) %copy-start.4) | copy-done | bytes 262168
  5.9 0.0 copy-start.5
  5.9 0.9 %copy-done.5 = f32[192,128]{1,0:T(8,128)S(1)} copy-done((f32[192,128]{1,0:T(8,128)S(1)}, f32[192,128]{1,0:T(8,128)}, u32[]{:S(2)}) %copy-start.5) | copy-done | bytes 98328
  6.8 0.0 copy-start.6
  6.8 0.7 copy-done.6
  7.5 70.5 %spectral_step.1 = (f32[16,32,128]{2,1,0:T(8,128)S(1)}, f32[16,32,128]{2,1,0:T(8,128)S(1)}, f32[16,32,128]{2,1,0:T(8,128)S(1)}) custom-call(f32[16,32,128]{2,1,0:T(8,128)S(1)} %copy-done.2, f32[3,16,32,128]{3,2,1,0:T(8,128)S(1)} %copy-done.1, f32[16,32,128]{2,1,0:T(8,128)S(1)} %copy-done.3, f32[16,32,128]{2,1,0:T(8,128)S(1)} %copy-done.4, ...), custom_call_target="tpu_custom_call" | custom-call | tf_op jit(solution)/shard_map/spectral_step/pallas_call | solution.py:653
  78.0 0.7 copy.13
  78.7 0.7 copy.14
  79.4 0.7 copy.15
Async XLA Ops:
  0.6 1.3 %copy-start = (bf16[9,256,256]{2,1,0:T(8,128)(2,1)S(1)}, bf16[9,256,256]{2,1,0:T(8,128)(2,1)}, u32[]{:S(2)}) copy-start(bf16[9,256,256]{2,1,0:T(8,128)(2,1)} %constant.4.clone.mats_ref) | copy-start | bytes 3538948
  1.9 1.1 %copy-start.1 = (f32[3,16,32,128]{3,2,1,0:T(8,128)S(1)}, f32[3,16,32,128]{3,2,1,0:T(8,128)}, u32[]{:S(2)}) copy-start(f32[3,16,32,128]{3,2,1,0:T(8,128)} %flow_hbm.1) | copy-start | bytes 2359300
  3.0 0.9 %copy-start.2 = (f32[16,32,128]{2,1,0:T(8,128)S(1)}, f32[16,32,128]{2,1,0:T(8,128)}, u32[]{:S(2)}) copy-start(f32[16,32,128]{2,1,0:T(8,128)} %temp_hbm.1) | copy-start | bytes 786436
  4.0 0.9 %copy-start.3 = (f32[16,32,128]{2,1,0:T(8,128)S(1)}, f32[16,32,128]{2,1,0:T(8,128)}, u32[]{:S(2)}) copy-start(f32[16,32,128]{2,1,0:T(8,128)} %cond_hbm.1) | copy-start | bytes 786436
  4.9 0.9 %copy-start.4 = (f32[16,32,128]{2,1,0:T(8,128)S(1)}, f32[16,32,128]{2,1,0:T(8,128)}, u32[]{:S(2)}) copy-start(f32[16,32,128]{2,1,0:T(8,128)} %vol_hbm.1) | copy-start | bytes 786436
  5.9 0.9 %copy-start.5 = (f32[192,128]{1,0:T(8,128)S(1)}, f32[192,128]{1,0:T(8,128)}, u32[]{:S(2)}) copy-start(f32[192,128]{1,0:T(8,128)} %constant.5.clone.rows_ref) | copy-start | bytes 294916
  6.8 0.7 copy-start.6

commit v3 on v2

--- a/solution.py
+++ b/solution.py
@@ -122,9 +122,9 @@
     flow_hbm,
     cond_hbm,
     vol_hbm,
-    off_ref,
-    mats_ref,
-    rows_ref,
+    off_hbm,
+    mats_hbm,
+    rows_hbm,
     newt_ref,
     press_ref,
     resid_ref,
@@ -132,6 +132,9 @@
     flow_ref,
     cond_ref,
     vol_ref,
+    off_ref,
+    mats_ref,
+    rows_ref,
     in_sem,
     weight,
     coef,
@@ -169,6 +172,9 @@
         pltpu.make_async_copy(a, b, in_sem.at[n])
         for n, (a, b) in enumerate(
             (
+                (rows_hbm, rows_ref),
+                (off_hbm, off_ref),
+                (mats_hbm, mats_ref),
                 (temp_hbm, temp_ref),
                 (flow_hbm, flow_ref),
                 (cond_hbm, cond_ref),
@@ -212,6 +218,7 @@
     y_up = (row_y % 8 == 7) & (row_y < ly - 1)
     y_down = (row_y % 8 == 0) & (row_y > 0)
 
+    loads[0].wait()
     wyz = rows_ref[0:ly]
     for x in range(lx):
         weight[x] = wyz * float(weights[x % 8])
@@ -441,12 +448,13 @@
         return cgrid[...]
 
     first = PITERS
+    loads[1].wait()
     ctile[...] = jnp.zeros((8, 128), F32)
     for ex in range(bx):
         ctile[ex * by : ex * by + by, 0:bz] = off_ref[ex]
     spread_out = jnp.where((from_lane < bz) & (from_lane == to_lane % bz), 1.0, 0.0).astype(F32)
     off_tile = dot(ctile[...], spread_out)
-    for load in loads:
+    for load in loads[2:]:
         load.wait()
     coef[...] = weight[...] * vol_ref[...]
 
@@ -551,10 +559,10 @@
             made.append(assemble_block(out + HELM_SHIFT * block(weight, b) * v))
         begin(slot, made)
         finish(slot)
-        resid_ref[...] = resid_ref[...] - part[slot]
 
         @pl.when(k == SMOOTH - 1)
         def _():
+            resid_ref[...] = resid_ref[...] - part[slot]
             turn = lax.div(t, cycle)
             sums = []
             for b in range(bx):
@@ -570,7 +578,10 @@
             along = along[0:count] + along[count : 2 * count] + along[2 * count :]
             wide = bdot(pxy[...], jnp.concatenate(narrow(along, 3), axis=1))
             wide = wide[:, 0:lz] + wide[:, lz : 2 * lz] + wide[:, 2 * lz :]
-            direc[...] = wide.reshape(lx, ly, lz)
+            wide = wide.reshape(lx, ly, lz)
+            for x in range(lx):
+                direc[x] = wide[x]
+                press_ref[x] = press_ref[x] + wide[x]
 
         @pl.when(k != SMOOTH - 1)
         def _():
@@ -579,11 +590,13 @@
             for n, (a, b) in enumerate(steps):
                 alpha = jnp.where(k == n, jnp.float32(a), alpha)
                 beta = jnp.where(k == n, jnp.float32(b), beta)
-            direc[...] = alpha * direc[...] + beta * (resid_ref[...] * q[...])
-
-        @pl.when(t < total - 1)
-        def _():
-            press_ref[...] = press_ref[...] + direc[...]
+            taken = jnp.where(t < total - 1, jnp.float32(1.0), jnp.float32(0.0))
+            for x in range(lx):
+                r = resid_ref[x] - part[slot, x]
+                resid_ref[x] = r
+                d = alpha * direc[x] + beta * (r * q[x])
+                direc[x] = d
+                press_ref[x] = press_ref[x] + taken * d
 
         return carry
 
@@ -627,7 +640,10 @@
         pltpu.VMEM((3, lx, ly, lz), F32),
         pltpu.VMEM((lx, ly, lz), F32),
         pltpu.VMEM((lx, ly, lz), F32),
-        pltpu.SemaphoreType.DMA((4,)),
+        pltpu.VMEM(blocks, F32),
+        pltpu.VMEM(mats.shape, BF16),
+        pltpu.VMEM(table.shape, F32),
+        pltpu.SemaphoreType.DMA((7,)),
         pltpu.VMEM((lx, ly, lz), F32),
         pltpu.VMEM((lx, ly, lz), F32),
         pltpu.VMEM((lx, ly, lz), F32),
@@ -653,11 +669,11 @@
     return pl.pallas_call(
         functools.partial(kernel, sizes, blocks),
         out_shape=(cube, cube, cube),
-        in_specs=[hbm] * 4 + [vmem] * 3,
+        in_specs=[hbm] * 7,
         out_specs=(vmem, vmem, vmem),
         scratch_shapes=scratch,
         compiler_params=pltpu.CompilerParams(
-            collective_id=0, has_side_effects=True, vmem_limit_bytes=40 * 1024 * 1024
+            collective_id=0, has_side_effects=True, vmem_limit_bytes=62 * 1024 * 1024
         ),
         name="spectral_step",
     )(temp, flow, cond, vol, off, jnp.asarray(mats), jnp.asarray(table))

time: 80.4 us -> 76.2 us (0.948)
  local copies, waits for them, and re-layouts: 8.94 us -> 4.09 us
    unnamed x17 -> x5, local copies, waits for them, and re-layouts: 8.94 us -> 4.09 us
where the time goes in v3:
time: 76.2 us; the launch traced here: 76 us
  Pallas kernels  71.3 us (94%)
  local copies, waits for them, and re-layouts  4.09 us (5%)
    pallas_call x1, Pallas kernels, shards(): pl.pallas_call(functools.partial(kernel, sizes, blocks), out_shape=(cube,...  71.3 us
    unnamed x5, local copies, waits for them, and re-layouts  4.09 us

profile of v3, /device:TPU:0, one launch (start us, length us, event | category | flops | bytes accessed | tf_op | source)
XLA Modules:
  0.0 76.0 jit_solution(6485950658916138429)
XLA Ops:
  0.6 71.3 %spectral_step.1 = (f32[16,32,128]{2,1,0:T(8,128)}, f32[16,32,128]{2,1,0:T(8,128)}, f32[16,32,128]{2,1,0:T(8,128)}) custom-call(f32[16,32,128]{2,1,0:T(8,128)} %temp_hbm.1, f32[3,16,32,128]{3,2,1,0:T(8,128)} %flow_hbm.1, f32[16,32,128]{2,1,0:T(8,128)} %cond_hbm.1, f32[16,32,128]{2,1,0:T(8,128)} %vol_hbm.1, f32[2,4,16]{2,1,0:T(4,128)} %off_hbm.1, ...), custom_call_target="tpu_custom_call" | custom-call | tf_op jit(solution)/shard_map/spectral_step/pallas_call | solution.py:669
  71.9 0.0 copy-start
  71.9 1.7 %copy.13 = f32[16,32,128]{2,1,0:T(8,128)} copy(f32[16,32,128]{2,1,0:T(8,128)} %get-tuple-element.6) | data formatting | bytes 524288
  73.6 1.7 %copy.14 = f32[16,32,128]{2,1,0:T(8,128)} copy(f32[16,32,128]{2,1,0:T(8,128)} %get-tuple-element.7) | data formatting | bytes 524288
  75.3 0.0 copy-done
  75.3 0.7 copy.15
Async XLA Ops:
  71.9 3.4 %copy-start = (f32[16,32,128]{2,1,0:T(8,128)S(1)}, f32[16,32,128]{2,1,0:T(8,128)}, u32[]{:S(2)}) copy-start(f32[16,32,128]{2,1,0:T(8,128)} %get-tuple-element.8) | copy-start | bytes 786436
